TPU v7x, 32 devices: a whole 2x2x4 slice. The times are simulated.
32 devices in a mesh: batch: 8 (over z, y), chan: 4 (over x, core).
Axes of the slice: x: 2, y: 2, z: 4, core: 2. Of those that a mesh axis runs over, the one named last changes fastest.
Arguments:
- features: bfloat16 [16, 48, 48, 512], P('batch', None, None, 'chan'), may hold values from -54 to 54
- tile_split: int32 [16, 2], P('batch'), may hold values from 2 to 22
- out_grad: bfloat16 [16, 24, 24, 1024], P('batch', None, None, 'chan'), may hold values from -18 to 18
- w_down: bfloat16 [3, 3, 512, 1024], P(None, None, None, 'chan'), may hold values from -0.09375 to 0.09375
- gain_down: float32 [1024], P('chan'), may hold values from 0.1 to 1.9
- shift_down: float32 [1024], P('chan'), may hold values from -3 to 3
- w_split: bfloat16 [2, 1024, 512], P(None, None, 'chan'), may hold values from -0.1875 to 0.1875
- gain_split: float32 [2, 512], P(None, 'chan'), may hold values from 0.1 to 1.9
- shift_split: float32 [2, 512], P(None, 'chan'), may hold values from -3 to 3
- w_first: bfloat16 [2, 512, 512], P(None, None, 'chan'), may hold values from -0.25 to 0.25
- w_second: bfloat16 [2, 3, 3, 512, 512], P(None, None, None, None, 'chan'), may hold values from -0.09375 to 0.09375
- gain_block: float32 [2, 2, 512], P(None, None, 'chan'), may hold values from 0.1 to 1.9
- shift_block: float32 [2, 2, 512], P(None, None, 'chan'), may hold values from -3 to 3
- w_trans: bfloat16 [512, 512], P(None, 'chan'), may hold values from -0.25 to 0.25
- gain_trans: float32 [512], P('chan'), may hold values from 0.1 to 1.9
- shift_trans: float32 [512], P('chan'), may hold values from -3 to 3
- w_merge: bfloat16 [1024, 1024], P(None, 'chan'), may hold values from -0.1875 to 0.1875
- gain_merge: float32 [1024], P('chan'), may hold values from 0.1 to 1.9
- shift_merge: float32 [1024], P('chan'), may hold values from -3 to 3
Outputs:
- mixed: bfloat16 [16, 24, 24, 1024], P('batch', None, None, 'chan')
- features_grad: float32 [16, 48, 48, 512], P('batch', None, None, 'chan')
- w_down_grad: float32 [3, 3, 512, 1024], P(None, None, None, 'chan')
- gain_down_grad: float32 [1024], P('chan')
- shift_down_grad: float32 [1024], P('chan')
- w_split_grad: float32 [2, 1024, 512], P(None, None, 'chan')
- gain_split_grad: float32 [2, 512], P(None, 'chan')
- shift_split_grad: float32 [2, 512], P(None, 'chan')
- w_first_grad: float32 [2, 512, 512], P(None, None, 'chan')
- w_second_grad: float32 [2, 3, 3, 512, 512], P(None, None, None, None, 'chan')
- gain_block_grad: float32 [2, 2, 512], P(None, None, 'chan')
- shift_block_grad: float32 [2, 2, 512], P(None, None, 'chan')
- w_trans_grad: float32 [512, 512], P(None, 'chan')
- gain_trans_grad: float32 [512], P('chan')
- shift_trans_grad: float32 [512], P('chan')
- w_merge_grad: float32 [1024, 1024], P(None, 'chan')
- gain_merge_grad: float32 [1024], P('chan')
- shift_merge_grad: float32 [1024], P('chan')
All inputs are finite; a program needn't handle non-finite values.
Results may differ from a plain program's by a relative error of at most 0.03.
Values may be sent and summed in bfloat16 or wider, within the bound.
A program may use at most 320 MiB of HBM per device.

v0:
```python
import functools

import jax
import jax.numpy as jnp
from jax import lax
from jax.experimental import pallas as pl
from jax.experimental.pallas import tpu as pltpu
from jax.sharding import PartitionSpec as P

epsilon = 1e-05
F32 = jnp.float32
BF16 = jnp.bfloat16
MESH = pl.DeviceIdType.MESH
LANES = 128
VMEM_LIMIT = 60 * 1024 * 1024


def tap_masks(splits, side_len, stride):
    places = jnp.arange(side_len, dtype=jnp.int32)
    offset = jnp.arange(3, dtype=jnp.int32) - 1
    source = stride * places[:, None] + offset[None, :]
    inside = (source >= 0) & (source < stride * side_len)

    def along_axis(cut_at):
        cut_at = cut_at[:, None, None]
        same_tile = (source[None] < stride * cut_at) == (places[None, :, None] < cut_at)
        return (inside[None] & same_tile).astype(jnp.float32)

    return (along_axis(splits[:, 0]), along_axis(splits[:, 1]))


def mask_columns(tile_split, side_len):
    number = tile_split.shape[0]
    rows_two, cols_two = tap_masks(tile_split, side_len, 2)
    rows_one, cols_one = tap_masks(tile_split, side_len, 1)

    def by_row(flags):
        return jnp.broadcast_to(flags[:, :, None], (number, side_len, side_len)).reshape(-1)

    def by_col(flags):
        return jnp.broadcast_to(flags[:, None, :], (number, side_len, side_len)).reshape(-1)

    stacked = jnp.stack(
        [
            by_row(rows_two[:, :, 0]),
            by_col(cols_two[:, :, 0]),
            by_row(rows_one[:, :, 0]),
            by_row(rows_one[:, :, 2]),
            by_col(cols_one[:, :, 0]),
            by_col(cols_one[:, :, 2]),
        ],
        axis=1,
    )
    return jnp.pad(stacked, ((side_len, side_len), (0, 2)))


class Places:
    def __init__(self, batch_count):
        self.count = batch_count
        self.chan = lax.axis_index("chan")
        self.batch = lax.axis_index("batch")
        self.mate = self.chan + 1 - 2 * lax.rem(self.chan, 2)
        self.cross = lax.rem(self.chan + 2, 4)
        self.far = lax.rem(self.mate + 2, 4)
        self.pair = self.chan // 2

    def greet(self):
        barrier = pltpu.get_barrier_semaphore()
        for partner in (self.mate, self.cross):
            pl.semaphore_signal(
                barrier, inc=1, device_id={"chan": partner}, device_id_type=MESH
            )

        def hail(step, carry):
            peer = lax.rem(self.batch + step, self.count)
            pl.semaphore_signal(barrier, inc=1, device_id={"batch": peer}, device_id_type=MESH)
            return carry

        lax.fori_loop(1, self.count, hail, 0)
        pl.semaphore_wait(barrier, 2 + self.count - 1)


class Gather:
    def __init__(self, places, view, chunks, send, recv, base):
        self.at, self.view, self.chunks = places, view, chunks
        self.send, self.recv, self.base = send, recv, base

    def copy(self, owner, chunk, kind, partner):
        ref = self.view(owner, chunk)
        slot = self.base + 3 * chunk + kind
        return pltpu.make_async_remote_copy(
            src_ref=ref,
            dst_ref=ref,
            send_sem=self.send.at[slot],
            recv_sem=self.recv.at[slot],
            device_id={"chan": partner},
            device_id_type=MESH,
        )

    def start(self, chunk):
        self.copy(self.at.chan, chunk, 1, self.at.cross).start()
        self.copy(self.at.chan, chunk, 0, self.at.mate).start()

    def wait_mate(self, chunk):
        self.copy(self.at.mate, chunk, 0, self.at.mate).wait_recv()

    def forward(self, chunk):
        self.copy(self.at.cross, chunk, 1, self.at.cross).wait_recv()
        self.copy(self.at.cross, chunk, 2, self.at.mate).start()

    def wait_far(self, chunk):
        self.copy(self.at.far, chunk, 2, self.at.mate).wait_recv()

    def drain(self):
        for chunk in range(self.chunks):
            self.copy(self.at.chan, chunk, 0, self.at.mate).wait_send()
            self.copy(self.at.chan, chunk, 1, self.at.cross).wait_send()
            self.copy(self.at.cross, chunk, 2, self.at.mate).wait_send()


class Exchange:
    def __init__(self, places, slots, send, recv):
        self.at, self.slots, self.send, self.recv = places, slots, send, recv

    def copy(self, step, owner, peer):
        ref = self.slots.at[owner]
        return pltpu.make_async_remote_copy(
            src_ref=ref,
            dst_ref=ref,
            send_sem=self.send.at[step],
            recv_sem=self.recv.at[step],
            device_id={"batch": peer},
            device_id_type=MESH,
        )

    def push(self, block):
        at = self.at
        self.slots[at.batch] = block

        def start(step, carry):
            self.copy(step, at.batch, lax.rem(at.batch + step, at.count)).start()
            return carry

        lax.fori_loop(1, at.count, start, 0)

    def take(self):
        at = self.at

        def arrive(step, carry):
            owner = lax.rem(at.batch + at.count - step, at.count)
            self.copy(step, owner, owner).wait_recv()
            return carry

        lax.fori_loop(1, at.count, arrive, 0)

    def drain(self):
        at = self.at

        def sent(step, carry):
            self.copy(step, at.batch, lax.rem(at.batch + step, at.count)).wait_send()
            return carry

        lax.fori_loop(1, at.count, sent, 0)


def two_rows(first, second):
    return jnp.where(
        lax.broadcasted_iota(jnp.int32, (8, first.shape[1]), 0) == 0, first, second
    )


def fold(values):
    return jnp.sum(values.reshape(values.shape[0] // 8, 8, values.shape[1]), axis=0)


def tiles(total, size, body):
    def step(index, carry):
        body(pl.multiple_of(index * size, size))
        return carry

    lax.fori_loop(0, total // size, step, 0)


def mish_parts(before):
    grown = jnp.exp(jnp.minimum(before, 20.0))
    top = grown * (grown + 2.0)
    return grown, top


def join(halves):
    return jnp.concatenate(halves, axis=1)


class Norms:
    def __init__(self, exchange, rows, pixels):
        self.exchange, self.rows, self.pixels = exchange, rows, pixels

    def statistics(self, z_ref):
        rows, width = self.rows, z_ref.shape[1]
        size = 96

        def add_up(index, total):
            return total + fold(z_ref[pl.ds(pl.multiple_of(index * size, size), size), :])

        zero = jnp.zeros((8, width), F32)
        total = lax.fori_loop(0, rows // size, add_up, zero)
        mean = jnp.sum(total, axis=0, keepdims=True) / rows

        def spread(index, total):
            away = z_ref[pl.ds(pl.multiple_of(index * size, size), size), :] - mean
            return total + fold(away * away)

        total = lax.fori_loop(0, rows // size, spread, zero)
        square = jnp.sum(total, axis=0, keepdims=True)
        self.exchange.push(two_rows(mean, square))
        self.exchange.take()
        slots, count = self.exchange.slots, self.exchange.at.count

        def means(index, total):
            return total + slots[index]

        whole = lax.fori_loop(0, count, means, zero)[0:1] / count

        def squares(index, total):
            block = slots[index]
            away = block[0:1] - whole
            return total + block[1:2] + rows * (away * away)

        variance = lax.fori_loop(0, count, squares, jnp.zeros((1, width), F32)) / self.pixels
        return whole, lax.rsqrt(variance + epsilon)


def forward_kernel(
    batch_count,
    side,
    feat,
    flags,
    wd_in,
    ws_in,
    wf_in,
    w2_in,
    wt_in,
    wm_in,
    gain_d,
    shift_d,
    gain_s,
    shift_s,
    gain_b,
    shift_b,
    gain_t,
    shift_t,
    gain_m,
    shift_m,
    mixed,
    feat_out,
    down_out,
    half_out,
    join_out,
    wide_out,
    slim_out,
    inv_wide,
    inv_slim,
    wd,
    ws,
    wf,
    w2,
    wt,
    wm,
    raw,
    fbuf,
    dbuf,
    hbuf,
    jbuf,
    hat_wide,
    hat_slim,
    acc_wide,
    acc_slim,
    z_wide,
    z_slim,
    branch,
    slots_wide,
    slots_slim,
    wide_sem,
    slim_sem,
    wide_rsem,
    slim_rsem,
    send,
    recv,
    wsem,
    osem,
):
    at = Places(batch_count)
    me = at.chan
    rows = z_wide.shape[0]
    half_rows = rows // 2
    pixels = rows * batch_count
    area = side * side

    weight_copies = {}

    def bring(name, pairs):
        copies = []
        for source, target in pairs:
            slot = sum(len(done) for done in weight_copies.values()) + len(copies)
            copies.append(pltpu.make_async_copy(source, target, wsem.at[slot]))
        weight_copies[name] = copies
        for copy in copies:
            copy.start()

    def have(name):
        for copy in weight_copies[name]:
            copy.wait()

    bring("down", [(wd_in.at[tap], wd.at[tap]) for tap in range(9)])
    bring("split", [(ws_in.at[part], ws.at[:, pl.ds(LANES * part, LANES)]) for part in range(2)])
    for layer in range(2):
        bring(f"first{layer}", [(wf_in.at[layer], wf.at[layer])])
        bring(
            f"second{layer}",
            [
                (w2_in.at[layer, tap], w2.at[layer, :, pl.ds(LANES * tap, LANES)])
                for tap in range(9)
            ],
        )
    bring("trans", [(wt_in, wt)])
    bring("merge", [(wm_in, wm)])

    saved = []

    def save(source, target):
        copy = pltpu.make_async_copy(source, target, osem.at[len(saved)])
        copy.start()
        saved.append(copy)

    base = [0]

    def gather(view, chunks):
        made = Gather(at, view, chunks, send, recv, base[0])
        base[0] += 3 * chunks
        return made

    def by_half(ref):
        return lambda owner, chunk: ref.at[owner, pl.ds(chunk * half_rows, half_rows)]

    feat_go = gather(lambda owner, phase: fbuf.at[owner, phase], 4)
    down_go = gather(by_half(dbuf), 2)
    half_go = [gather(by_half(hbuf.at[index]), 2) for index in range(5)]
    side_go = gather(by_half(jbuf.at[1]), 2)
    top_go = gather(by_half(jbuf.at[0]), 2)
    wide_ex = [
        Exchange(at, slots_wide.at[index], wide_sem.at[index], wide_rsem.at[index])
        for index in range(3)
    ]
    slim_ex = [
        Exchange(at, slots_slim.at[index], slim_sem.at[index], slim_rsem.at[index])
        for index in range(5)
    ]

    at.greet()

    for phase in range(4):
        row_par, col_par = phase // 2, phase % 2

        if col_par == 0:

            def widen(index, carry):
                raw[index] = feat[2 * index + row_par].astype(F32)
                return carry

            lax.fori_loop(0, feat.shape[0] // 2, widen, 0)

        def pick(start):
            both = [
                raw[2 * (start // (2 * side)) + step, pl.ds(col_par, side, stride=2), :]
                for step in range(2)
            ]
            fbuf[me, phase, pl.ds(start, 2 * side), :] = jnp.concatenate(both, axis=0).astype(BF16)

        tiles(rows, 2 * side, pick)
        feat_go.start(phase)

    acc_wide[...] = jnp.zeros_like(acc_wide)
    have("down")

    def down_pair(phase, pair):
        row_par, col_par = phase // 2, phase % 2
        row_taps = (0, 2) if row_par else (1,)
        col_taps = (0, 2) if col_par else (1,)
        size = 192

        def body(start):
            block = join(
                [fbuf[2 * pair + step, phase, pl.ds(start, size), :] for step in range(2)]
            )
            for row_tap in row_taps:
                for col_tap in col_taps:
                    part = jnp.dot(
                        block,
                        wd[3 * row_tap + col_tap, pl.ds(pl.multiple_of(pair * 256, 256), 256), :],
                        preferred_element_type=F32,
                    )
                    place = pl.ds(start + (2 * side if row_tap == 0 else side), size)
                    if row_tap == 0:
                        part = part * flags[place, 0:1]
                    kind = 1 if col_tap == 0 else 0
                    acc_wide[kind, place, :] += part

        tiles(rows, size, body)

    for phase in range(4):
        feat_go.wait_mate(phase)
        down_pair(phase, at.pair)
        feat_go.forward(phase)
    for phase in range(4):
        feat_go.wait_far(phase)
        down_pair(phase, 1 - at.pair)
    save(fbuf, feat_out)

    vsize = 4 * side

    def settle_down(start):
        place = pl.ds(start + side, vsize)
        z_wide[pl.ds(start, vsize), :] = acc_wide[0, place, :] + flags[place, 1:2] * pltpu.roll(
            acc_wide[1, place, :], 1, 0
        )

    tiles(rows, vsize, settle_down)

    def activate(exchange, z_ref, hat_ref, gain, shift, inv_ref, give, begin):
        mean, inverse = Norms(exchange, rows, pixels).statistics(z_ref)
        inv_ref[...] = jnp.broadcast_to(inverse, inv_ref.shape)

        def body(start):
            place = pl.ds(start, vsize)
            normed = (z_ref[place, :] - mean) * inverse
            hat_ref[place, :] = normed
            before = normed * gain + shift
            _, top = mish_parts(before)
            give(place, before * (top / (top + 2.0)))

        for chunk in range(2):

            def inner(start):
                body(start + chunk * half_rows)

            tiles(half_rows, vsize, inner)
            begin(chunk)

    def keep_down(place, value):
        dbuf[me, place, :] = value.astype(BF16)

    activate(
        wide_ex[0], z_wide, hat_wide.at[0], gain_d[...], shift_d[...], inv_wide.at[0], keep_down,
        down_go.start,
    )
    save(hat_wide.at[0], wide_out.at[0])
    have("split")

    msize = 192

    def split_block(owner, chunk, first):
        def body(start):
            place = pl.ds(start + chunk * half_rows, msize)
            part = jnp.dot(
                dbuf[owner, place, :],
                ws[pl.ds(pl.multiple_of(owner * 256, 256), 256), :],
                preferred_element_type=F32,
            )
            if first:
                z_wide[place, :] = part
            else:
                z_wide[place, :] += part

        tiles(half_rows, msize, body)

    for chunk in range(2):
        split_block(me, chunk, True)
    for chunk in range(2):
        down_go.wait_mate(chunk)
        split_block(at.mate, chunk, False)
    for chunk in range(2):
        down_go.forward(chunk)
        split_block(at.cross, chunk, False)
    for chunk in range(2):
        down_go.wait_far(chunk)
        split_block(at.far, chunk, False)
    save(dbuf, down_out)

    def keep_split(place, value):
        branch[place, :] = value[:, :LANES]
        hbuf[0, me, place, :] = value[:, :LANES].astype(BF16)
        jbuf[1, me, place, :] = value[:, LANES:].astype(BF16)

    activate(
        wide_ex[1],
        z_wide,
        hat_wide.at[1],
        join([gain_s[0:1, :], gain_s[1:2, :]]),
        join([shift_s[0:1, :], shift_s[1:2, :]]),
        inv_wide.at[1],
        keep_split,
        half_go[0].start,
    )
    save(hat_wide.at[1], wide_out.at[1])
    for chunk in range(2):
        side_go.start(chunk)

    def two_of(ref, pair, place):
        return join([ref[2 * pair + step, place, :] for step in range(2)])

    def thin_pair(source, weight, pair, chunk, first):
        def body(start):
            place = pl.ds(start + chunk * half_rows, msize)
            part = jnp.dot(
                two_of(source, pair, place),
                weight[pl.ds(pl.multiple_of(pair * 256, 256), 256), :],
                preferred_element_type=F32,
            )
            if first:
                z_slim[place, :] = part
            else:
                z_slim[place, :] += part

        tiles(half_rows, msize, body)

    def thin_conv(index, weight):
        source, go = hbuf.at[index], half_go[index]
        for chunk in range(2):
            go.wait_mate(chunk)
            thin_pair(source, weight, at.pair, chunk, True)
        for chunk in range(2):
            go.forward(chunk)
        for chunk in range(2):
            go.wait_far(chunk)
            thin_pair(source, weight, 1 - at.pair, chunk, False)
        save(source, half_out.at[index])

    def tap_pair(source, weight, pair, chunk):
        def body(start):
            begin = start + chunk * half_rows
            part = jnp.dot(
                two_of(source, pair, pl.ds(begin, msize)),
                weight[pl.ds(pl.multiple_of(pair * 256, 256), 256), :],
                preferred_element_type=F32,
            )
            for col_tap in range(3):
                for row_tap in range(3):
                    tap = 3 * row_tap + col_tap
                    piece = part[:, LANES * tap : LANES * (tap + 1)]
                    place = pl.ds(begin + side - side * (row_tap - 1), msize)
                    if row_tap != 1:
                        column = 2 if row_tap == 0 else 3
                        piece = piece * flags[place, column : column + 1]
                    acc_slim[col_tap, place, :] += piece

        tiles(half_rows, msize, body)

    def tap_conv(index, weight):
        source, go = hbuf.at[index], half_go[index]
        acc_slim[...] = jnp.zeros_like(acc_slim)
        for chunk in range(2):
            go.wait_mate(chunk)
            tap_pair(source, weight, at.pair, chunk)
        for chunk in range(2):
            go.forward(chunk)
        for chunk in range(2):
            go.wait_far(chunk)
            tap_pair(source, weight, 1 - at.pair, chunk)
        save(source, half_out.at[index])

        def settle(start):
            place = pl.ds(start + side, vsize)
            z_slim[pl.ds(start, vsize), :] = (
                acc_slim[1, place, :]
                + flags[place, 4:5] * pltpu.roll(acc_slim[0, place, :], 1, 0)
                + flags[place, 5:6] * pltpu.roll(acc_slim[2, place, :], vsize - 1, 0)
            )

        tiles(rows, vsize, settle)

    def slim_act(index, gain, shift, give, begin):
        activate(
            slim_ex[index], z_slim, hat_slim.at[index], gain, shift, inv_slim.at[index], give, begin
        )
        save(hat_slim.at[index], slim_out.at[index])

    for layer in range(2):
        have(f"first{layer}")
        thin_conv(2 * layer, wf.at[layer])

        def keep_inner(place, value):
            hbuf[2 * layer + 1, me, place, :] = value.astype(BF16)

        slim_act(
            2 * layer,
            gain_b[2 * layer : 2 * layer + 1, :],
            shift_b[2 * layer : 2 * layer + 1, :],
            keep_inner,
            half_go[2 * layer + 1].start,
        )
        have(f"second{layer}")
        tap_conv(2 * layer + 1, w2.at[layer])

        def keep_branch(place, value):
            total = branch[place, :] + value
            branch[place, :] = total
            hbuf[2 * layer + 2, me, place, :] = total.astype(BF16)

        slim_act(
            2 * layer + 1,
            gain_b[2 * layer + 1 : 2 * layer + 2, :],
            shift_b[2 * layer + 1 : 2 * layer + 2, :],
            keep_branch,
            half_go[2 * layer + 2].start,
        )
        if layer == 0:
            for chunk in range(2):
                side_go.forward(chunk)
    have("trans")
    thin_conv(4, wt)

    def keep_top(place, value):
        jbuf[0, me, place, :] = value.astype(BF16)

    slim_act(4, gain_t[...], shift_t[...], keep_top, top_go.start)
    have("merge")

    def merge_pair(part_index, pair, chunk, first):
        def body(start):
            place = pl.ds(start + chunk * half_rows, msize)
            part = jnp.dot(
                two_of(jbuf.at[part_index], pair, place),
                wm[pl.ds(pl.multiple_of(part_index * 512 + pair * 256, 256), 256), :],
                preferred_element_type=F32,
            )
            if first:
                z_wide[place, :] = part
            else:
                z_wide[place, :] += part

        tiles(half_rows, msize, body)

    for chunk in range(2):
        side_go.wait_mate(chunk)
        merge_pair(1, at.pair, chunk, True)
    for chunk in range(2):
        side_go.wait_far(chunk)
        merge_pair(1, 1 - at.pair, chunk, False)
    for chunk in range(2):
        top_go.wait_mate(chunk)
        merge_pair(0, at.pair, chunk, False)
    for chunk in range(2):
        top_go.forward(chunk)
    for chunk in range(2):
        top_go.wait_far(chunk)
        merge_pair(0, 1 - at.pair, chunk, False)
    save(jbuf, join_out)

    def keep_mixed(place, value):
        mixed[place, :] = value.astype(BF16)

    activate(
        wide_ex[2], z_wide, hat_wide.at[2], gain_m[...], shift_m[...], inv_wide.at[2], keep_mixed,
        lambda chunk: None,
    )
    save(hat_wide.at[2], wide_out.at[2])

    for made in (feat_go, down_go, *half_go, side_go, top_go):
        made.drain()
    for made in (*wide_ex, *slim_ex):
        made.drain()
    for copy in saved:
        copy.wait()


def forward_call(batch_count, side, feat, flags, weights, vectors):
    rows = feat.shape[0] * side // 2
    wide = 2 * LANES
    hbm = pl.BlockSpec(memory_space=pl.ANY)
    vmem = pl.BlockSpec(memory_space=pltpu.VMEM)
    dma = pltpu.SemaphoreType.DMA
    shape = jax.ShapeDtypeStruct
    kept = [
        shape((4, 4, rows, LANES), BF16),
        shape((4, rows, wide), BF16),
        shape((5, 4, rows, LANES), BF16),
        shape((2, 4, rows, LANES), BF16),
        shape((3, rows, wide), F32),
        shape((5, rows, LANES), F32),
    ]
    taps_width = 9 * LANES
    scratch = [
        pltpu.VMEM((9, 512, wide), BF16),
        pltpu.VMEM((1024, wide), BF16),
        pltpu.VMEM((2, 512, LANES), BF16),
        pltpu.VMEM((2, 512, taps_width), BF16),
        pltpu.VMEM((512, LANES), BF16),
        pltpu.VMEM((1024, wide), BF16),
        pltpu.VMEM((feat.shape[0] // 2, feat.shape[1], LANES), F32),
        *[pltpu.VMEM(one.shape, one.dtype) for one in kept],
        pltpu.VMEM((2, rows + 2 * side, wide), F32),
        pltpu.VMEM((3, rows + 2 * side, LANES), F32),
        pltpu.VMEM((rows, wide), F32),
        pltpu.VMEM((rows, LANES), F32),
        pltpu.VMEM((rows, LANES), F32),
        pltpu.VMEM((3, batch_count, 8, wide), F32),
        pltpu.VMEM((5, batch_count, 8, LANES), F32),
        dma((3, batch_count)),
        dma((5, batch_count)),
        dma((3, batch_count)),
        dma((5, batch_count)),
        dma((60,)),
        dma((60,)),
        dma((40,)),
        dma((20,)),
    ]
    return pl.pallas_call(
        functools.partial(forward_kernel, batch_count, side),
        out_shape=[
            shape((rows, wide), BF16),
            *kept,
            shape((3, 8, wide), F32),
            shape((5, 8, LANES), F32),
        ],
        in_specs=[vmem, vmem] + [hbm] * 6 + [vmem] * 10,
        out_specs=[vmem] + [hbm] * 6 + [vmem, vmem],
        scratch_shapes=scratch,
        compiler_params=pltpu.CompilerParams(
            collective_id=0, has_side_effects=True, vmem_limit_bytes=VMEM_LIMIT
        ),
    )(feat, flags, *weights, *vectors)


class Scatter:
    def __init__(self, places, views, send, recv, base):
        self.at = places
        self.term, self.from_mate, self.from_cross, self.across = views
        self.send, self.recv, self.base = send, recv, base
        self.used = []

    def copy(self, source, target, chunk, kind, partner):
        slot = self.base + 3 * chunk + kind
        return pltpu.make_async_remote_copy(
            src_ref=source,
            dst_ref=target,
            send_sem=self.send.at[slot],
            recv_sem=self.recv.at[slot],
            device_id={"chan": partner},
            device_id_type=MESH,
        )

    def far_copy(self, chunk):
        return self.copy(
            self.term(self.at.far, chunk), self.from_mate(0, chunk), chunk, 0, self.at.mate
        )

    def mate_copy(self, chunk):
        return self.copy(
            self.term(self.at.mate, chunk), self.from_mate(1, chunk), chunk, 1, self.at.mate
        )

    def cross_copy(self, chunk):
        return self.copy(self.across(chunk), self.from_cross(chunk), chunk, 2, self.at.cross)

    def relay(self, chunk, size):
        self.far_copy(chunk).wait_recv()
        mine, theirs, both = (
            self.term(self.at.cross, chunk),
            self.from_mate(0, chunk),
            self.across(chunk),
        )

        def add(start):
            place = pl.ds(start, size)
            both[place, :] = (mine[place, :].astype(F32) + theirs[place, :].astype(F32)).astype(
                BF16
            )

        tiles(mine.shape[0], size, add)
        self.cross_copy(chunk).start()

    def finish(self, chunk, size, give):
        self.mate_copy(chunk).wait_recv()
        self.cross_copy(chunk).wait_recv()
        parts = (self.term(self.at.chan, chunk), self.from_mate(1, chunk), self.from_cross(chunk))

        def add(start):
            place = pl.ds(start, size)
            first, second, third = [part[place, :].astype(F32) for part in parts]
            give(start, first + second + third)

        tiles(parts[0].shape[0], size, add)
        self.used.append(chunk)

    def drain(self):
        for chunk in self.used:
            self.far_copy(chunk).wait_send()
            self.mate_copy(chunk).wait_send()
            self.cross_copy(chunk).wait_send()


def tile_of(rows):
    return max(size for size in range(8, 321, 8) if rows % size == 0)


class Reducer:
    def __init__(self, places, buf, landing, out, order, sems, base, own_sem):
        self.at, self.buf, self.landing, self.out = places, buf, landing, out
        self.order, (self.send, self.recv), self.base = order, sems, base
        self.own_sem = own_sem
        self.low, self.size, self.taken, self.step = 0, buf.shape[0], 0, 0

    def partner(self, bit):
        side = lax.rem(self.at.batch // (1 << bit), 2)
        return side, self.at.batch + (1 - 2 * side) * (1 << bit)

    def copy(self, source, target, partner):
        return pltpu.make_async_remote_copy(
            src_ref=source,
            dst_ref=target,
            send_sem=self.send.at[self.base + self.step],
            recv_sem=self.recv.at[self.base + self.step],
            device_id={"batch": partner},
            device_id_type=MESH,
        )

    def rows(self, low, size):
        return pl.ds(pl.multiple_of(low, 8), size)

    def launch(self):
        steps = len(self.order)
        if self.step < steps:
            side, partner = self.partner(self.order[self.step])
            half = self.size // 2
            gone = self.low + (1 - side) * half
            self.flying = self.copy(
                self.buf.at[self.rows(gone, half)],
                self.landing.at[pl.ds(self.taken, half)],
                partner,
            )
            self.kept = self.low + side * half
            self.flying.start()
            return
        side, partner = self.partner(self.order[2 * steps - 1 - self.step])
        target = self.out.at[self.rows(self.low, self.size)]
        source = target
        if self.step == steps:
            source = self.buf.at[self.rows(self.low, self.size)]
            self.own = pltpu.make_async_copy(source, target, self.own_sem)
            self.own.start()
        self.flying = self.copy(source, target, partner)
        self.flying.start()
        other = self.out.at[self.rows(self.low + (1 - 2 * side) * self.size, self.size)]
        self.coming = self.copy(other, other, partner)
        self.next_low = self.low - side * self.size

    def advance(self):
        steps = len(self.order)
        if self.step < steps:
            self.flying.wait()
            half = self.size // 2
            size = tile_of(half)
            taken, kept = self.taken, self.kept

            def add(start):
                place = self.rows(kept + start, size)
                self.buf[place, :] = (
                    self.buf[place, :].astype(F32)
                    + self.landing[pl.ds(taken + start, size), :].astype(F32)
                ).astype(BF16)

            tiles(half, size, add)
            self.low, self.size, self.taken = kept, half, taken + half
        else:
            self.coming.wait_recv()
            self.flying.wait_send()
            if self.step == steps:
                self.own.wait()
            self.low, self.size = self.next_low, 2 * self.size
        self.step += 1
        if self.step == 2 * steps:
            return True
        self.launch()
        return False


def landing_rows(rows, batch_count):
    return rows - rows // batch_count


def backward_kernel(
    batch_count,
    side,
    orders,
    grad_in,
    flags,
    wd_in,
    ws_in,
    wf_in,
    w2_in,
    wt_in,
    wm_in,
    feat_in,
    down_in,
    half_in,
    join_in,
    wide_in,
    slim_in,
    inv_wide,
    inv_slim,
    gain_d,
    shift_d,
    gain_s,
    shift_s,
    gain_b,
    shift_b,
    gain_t,
    shift_t,
    gain_m,
    shift_m,
    feat_grad,
    vec_wide,
    vec_slim,
    merge_out,
    late_out,
    early_out,
    split_out,
    down_out,
    grad,
    wd,
    ws,
    wf,
    w2,
    wt,
    wm,
    fbuf,
    dbuf,
    hbuf,
    jbuf,
    hat_wide,
    hat_slim,
    up_wide,
    up_slim,
    branch,
    bypass,
    shifted,
    spread,
    dz_wide,
    dz_slim,
    pbuf,
    rmate,
    rcross,
    across,
    rcross_d,
    across_d,
    sum_merge,
    sum_late,
    sum_early,
    sum_split,
    sum_down,
    land_merge,
    land_late,
    land_early,
    land_split,
    slots_wide,
    slots_slim,
    wide_sem,
    slim_sem,
    wide_rsem,
    slim_rsem,
    send,
    recv,
    bsend,
    brecv,
    wsem,
    osem,
):
    at = Places(batch_count)
    rows = up_wide.shape[0]
    half_rows = rows // 2
    pixels = rows * batch_count
    vsize = 4 * side
    msize = 192

    fetched = {}
    count = [0]

    def bring(name, *pairs):
        copies = []
        for source, target in pairs:
            copies.append(pltpu.make_async_copy(source, target, wsem.at[count[0]]))
            count[0] += 1
        fetched[name] = copies
        for copy in copies:
            copy.start()

    def have(name):
        for copy in fetched[name]:
            copy.wait()

    bring("grad", (grad_in, grad), (wide_in.at[2], hat_wide.at[2]))
    bring("merge", (wm_in, wm))
    bring("joined", (join_in, jbuf))
    bring("hat4", (slim_in.at[4], hat_slim.at[4]))
    bring("trans", (wt_in, wt))
    bring("half4", (half_in.at[4], hbuf.at[4]))
    for layer in (1, 0):
        index = 2 * layer + 1
        bring(f"hat{index}", (slim_in.at[index], hat_slim.at[index]))
        bring(
            f"second{layer}",
            *[
                (w2_in.at[layer, tap], w2.at[layer, :, pl.ds(LANES * tap, LANES)])
                for tap in range(9)
            ],
        )
        bring(f"half{index}", (half_in.at[index], hbuf.at[index]))
        index = 2 * layer
        bring(f"hat{index}", (slim_in.at[index], hat_slim.at[index]))
        bring(f"first{layer}", (wf_in.at[layer], wf.at[layer]))
        bring(f"half{index}", (half_in.at[index], hbuf.at[index]))
    bring("hat_split", (wide_in.at[1], hat_wide.at[1]))
    bring("split", *[(ws_in.at[part], ws.at[:, pl.ds(LANES * part, LANES)]) for part in range(2)])
    bring("down_low", (down_in, dbuf))
    bring("hat_down", (wide_in.at[0], hat_wide.at[0]))
    bring("features", (feat_in, fbuf))
    bring("down", *[(wd_in.at[tap], wd.at[tap]) for tap in range(9)])

    wide_ex = [
        Exchange(at, slots_wide.at[index], wide_sem.at[index], wide_rsem.at[index])
        for index in range(3)
    ]
    slim_ex = [
        Exchange(at, slots_slim.at[index], slim_sem.at[index], slim_rsem.at[index])
        for index in range(5)
    ]

    base = [0]

    def scatter(stage, parts):
        kit = stage % 2

        def cut(ref):
            return lambda *where: ref.at[(*where[:-1], pl.ds(where[-1] * half_rows, half_rows))]

        def term(owner, chunk):
            return cut(pbuf)(chunk // 2, owner, chunk % 2)

        def from_mate(block, chunk):
            return cut(rmate)(kit, chunk // 2, block, chunk % 2)

        def from_cross(chunk):
            return cut(rcross)(kit, chunk // 2, chunk % 2)

        def over(chunk):
            return cut(across)(chunk // 2, chunk % 2)

        made = Scatter(at, (term, from_mate, from_cross, over), send, recv, base[0])
        base[0] += 6 * parts
        return made

    steps = 2 * len(orders[0])
    bbase = [0]

    queue = []

    def begin(buf, landing, order, out):
        made = Reducer(
            at,
            buf,
            landing,
            out,
            orders[order],
            (bsend, brecv),
            bbase[0],
            osem.at[bbase[0] // steps],
        )
        bbase[0] += steps
        made.launch()
        queue.append(made)

    def tick(most=1):
        for made in list(queue)[:most]:
            if made.advance():
                queue.remove(made)

    at.greet()

    for ref in (shifted,):
        ref[...] = jnp.zeros_like(ref)

    def norm_back(exchange, load, back, hat, gain, shift, inverse, vec_ref, give, meanwhile):
        width = back.shape[1]

        def first(index, carry):
            place = pl.ds(pl.multiple_of(index * vsize, vsize), vsize)
            normed = hat[place, :]
            before = normed * gain + shift
            grown, top = mish_parts(before)
            share = 1.0 / (top + 2.0)
            slope = top * share + before * (4.0 * grown * (1.0 + grown) * share * share)
            value = load(place) * slope
            back[place, :] = value
            return (carry[0] + fold(value), carry[1] + fold(value * normed))

        zero = jnp.zeros((8, width), F32)
        one, two = lax.fori_loop(0, rows // vsize, first, (zero, zero))
        exchange.push(
            two_rows(jnp.sum(one, axis=0, keepdims=True), jnp.sum(two, axis=0, keepdims=True))
        )
        meanwhile()
        exchange.take()
        slots = exchange.slots

        def gather_up(index, total):
            return total + slots[index]

        total = lax.fori_loop(0, batch_count, gather_up, zero)
        vec_ref[...] = total
        scale = gain * inverse
        shift_part, gain_part = total[0:1] / pixels, total[1:2] / pixels

        def second(start):
            place = pl.ds(start, vsize)
            give(start, scale * (back[place, :] - shift_part - hat[place, :] * gain_part))

        tiles(rows, vsize, second)

    across_dims = (((1,), (1,)), ((), ()))
    along_dims = (((0,), (0,)), ((), ()))

    def back_pair(left, weight, pair, chunk, part):
        def body(start):
            begin_at = start + chunk * half_rows
            terms = lax.dot_general(
                left(pl.ds(begin_at, msize)), weight, across_dims, preferred_element_type=F32
            ).astype(BF16)
            for step in range(2):
                pbuf[part, 2 * pair + step, pl.ds(begin_at, msize), :] = terms[
                    :, LANES * step : LANES * (step + 1)
                ]

        tiles(half_rows, msize, body)

    def pair_rows(pair, offset=0):
        return pl.ds(pl.multiple_of(offset + pair * 256, 256), 256)

    def spread_out(go, left, weight_at, parts):
        chunks = 2 * parts
        for chunk in range(chunks):
            back_pair(left, weight_at(chunk // 2, 1 - at.pair), 1 - at.pair, chunk % 2, chunk // 2)
            go.far_copy(chunk).start()
        for chunk in range(chunks):
            go.relay(chunk, vsize)
        for chunk in range(chunks):
            back_pair(left, weight_at(chunk // 2, at.pair), at.pair, chunk % 2, chunk // 2)
            go.mate_copy(chunk).start()

    def two_of(ref, pair):
        return join([ref[2 * pair + step] for step in range(2)])

    have("grad")
    merge_go = scatter(0, 2)

    def keep_wide(start, value):
        dz_wide[pl.ds(start, vsize), :] = value.astype(BF16)

    norm_back(
        wide_ex[2],
        lambda place: grad[place, :].astype(F32),
        up_wide,
        hat_wide.at[2],
        gain_m[...],
        shift_m[...],
        inv_wide[2, 0:1, :],
        vec_wide.at[2],
        keep_wide,
        lambda: None,
    )
    have("merge")
    spread_out(
        merge_go,
        lambda place: dz_wide[place, :],
        lambda part, pair: wm[pair_rows(pair, 512 * part), :],
        2,
    )
    have("joined")
    for part in range(2):
        for pair in range(2):
            sum_merge[pl.ds(512 * part + 256 * pair, 256), :] = lax.dot_general(
                two_of(jbuf.at[part], pair), dz_wide[...], along_dims, preferred_element_type=F32
            ).astype(BF16)
    begin(sum_merge, land_merge, 0, merge_out)

    def top_up(chunk):
        def give(start, value):
            up_slim[pl.ds(start + chunk * half_rows, vsize), :] = value

        return give

    for chunk in range(2):
        merge_go.finish(chunk, vsize, top_up(chunk))

    def keep_slim(start, value):
        dz_slim[pl.ds(start, vsize), :] = value.astype(BF16)

    def slim_back(index, load, gain, shift, give):
        have(f"hat{index}")
        norm_back(
            slim_ex[index],
            load,
            up_slim,
            hat_slim.at[index],
            gain,
            shift,
            inv_slim[index, 0:1, :],
            vec_slim.at[index],
            give,
            tick,
        )

    def thin_back(stage, index, weight, name, target, offset, settle, extra=None):
        go = scatter(stage, 1)
        have(name)
        spread_out(
            go,
            lambda place: dz_slim[place, :],
            lambda part, pair: weight[pair_rows(pair), :],
            1,
        )
        have(f"half{index}")
        for pair in range(2):
            target[pl.ds(offset + 256 * pair, 256), :] = lax.dot_general(
                two_of(hbuf.at[index], pair), dz_slim[...], along_dims, preferred_element_type=F32
            ).astype(BF16)
        if extra is not None:
            extra()
        tick()
        for chunk in range(2):
            go.finish(chunk, vsize, settle(chunk))
        return go

    slim_back(4, lambda place: up_slim[place, :], gain_t[...], shift_t[...], keep_slim)

    def branch_new(chunk):
        def give(start, value):
            branch[pl.ds(start + chunk * half_rows, vsize), :] = value

        return give

    def branch_more(chunk):
        def give(start, value):
            branch[pl.ds(start + chunk * half_rows, vsize), :] += value

        return give

    def bypass_up(chunk):
        def give(start, value):
            bypass[pl.ds(start + chunk * half_rows, vsize), :] = value

        return give

    def finish_bypass():
        for chunk in range(2):
            merge_go.finish(2 + chunk, vsize, bypass_up(chunk))
        merge_go.drain()

    finish_bypass()
    thin_back(1, 4, wt, "trans", sum_late, 4608, branch_new).drain()

    def nine(start, value):
        place = pl.ds(start + side, vsize)
        value = value.astype(BF16).astype(F32)
        shifted[1, place, :] = value
        shifted[0, place, :] = pltpu.roll(value * flags[place, 4:5], vsize - 1, 0)
        shifted[2, place, :] = pltpu.roll(value * flags[place, 5:6], 1, 0)

    def nine_rows(start):
        for row_tap in range(3):
            source = pl.ds(start + side - side * (row_tap - 1), vsize)
            for col_tap in range(3):
                tap = 3 * row_tap + col_tap
                value = shifted[col_tap, source, :]
                if row_tap != 1:
                    column = 2 if row_tap == 0 else 3
                    value = value * flags[source, column : column + 1]
                spread[pl.ds(start, vsize), LANES * tap : LANES * (tap + 1)] = value.astype(BF16)

    def tap_back(stage, layer, target, settle, extra):
        index = 2 * layer + 1
        go = scatter(stage, 1)
        tiles(rows, vsize, nine_rows)
        have(f"second{layer}")
        spread_out(
            go,
            lambda place: spread[place, :],
            lambda part, pair: w2[layer, pair_rows(pair), :],
            1,
        )
        have(f"half{index}")
        for pair in range(2):
            left = two_of(hbuf.at[index], pair)
            for row_tap in range(3):
                three = lax.dot_general(
                    left,
                    spread[:, 3 * LANES * row_tap : 3 * LANES * (row_tap + 1)],
                    along_dims,
                    preferred_element_type=F32,
                ).astype(BF16)
                for col_tap in range(3):
                    target[pl.ds(512 * (3 * row_tap + col_tap) + 256 * pair, 256), :] = three[
                        :, LANES * col_tap : LANES * (col_tap + 1)
                    ]
        extra()
        tick()
        for chunk in range(2):
            go.finish(chunk, vsize, settle(chunk))
        go.drain()

    for layer in (1, 0):
        stage = 2 if layer == 1 else 4
        target = sum_late if layer == 1 else sum_early
        slim_back(
            2 * layer + 1,
            lambda place: branch[place, :],
            gain_b[2 * layer + 1 : 2 * layer + 2, :],
            shift_b[2 * layer + 1 : 2 * layer + 2, :],
            nine,
        )
        if layer == 1:
            extra = lambda: begin(sum_late, land_late, 1, late_out)
        else:
            extra = lambda: begin(sum_early, land_early, 1, early_out)
        tap_back(stage, layer, target, top_up, extra)
        slim_back(
            2 * layer,
            lambda place: up_slim[place, :],
            gain_b[2 * layer : 2 * layer + 1, :],
            shift_b[2 * layer : 2 * layer + 1, :],
            keep_slim,
        )
        thin_back(
            stage + 1,
            2 * layer,
            wf.at[layer],
            f"first{layer}",
            sum_early if layer == 1 else sum_split,
            4608 if layer == 1 else 2048,
            branch_more,
        ).drain()

    have("hat_split")
    norm_back(
        wide_ex[1],
        lambda place: join([branch[place, :], bypass[place, :]]),
        up_wide,
        hat_wide.at[1],
        join([gain_s[0:1, :], gain_s[1:2, :]]),
        join([shift_s[0:1, :], shift_s[1:2, :]]),
        inv_wide[1, 0:1, :],
        vec_wide.at[1],
        keep_wide,
        tick,
    )
    have("split")
    split_go = scatter(6, 2)

    def split_terms(owner, chunk):
        def body(start):
            place = pl.ds(start + chunk * half_rows, msize)
            terms = lax.dot_general(
                dz_wide[place, :],
                ws[pl.ds(pl.multiple_of(owner * 256, 256), 256), :],
                across_dims,
                preferred_element_type=F32,
            ).astype(BF16)
            for part in range(2):
                pbuf[part, owner, place, :] = terms[:, LANES * part : LANES * (part + 1)]

        tiles(half_rows, msize, body)

    for chunk in range(2):
        split_terms(at.far, chunk)
        for part in range(2):
            split_go.far_copy(2 * part + chunk).start()
    for chunk in range(2):
        split_terms(at.cross, chunk)
        for part in range(2):
            split_go.relay(2 * part + chunk, vsize)
    for chunk in range(2):
        split_terms(at.mate, chunk)
        for part in range(2):
            split_go.mate_copy(2 * part + chunk).start()
    for chunk in range(2):
        split_terms(at.chan, chunk)
    have("down_low")
    for owner in range(4):
        result = lax.dot_general(
            dbuf[rows * owner : rows * (owner + 1), :], dz_wide[...], along_dims, preferred_element_type=F32
        ).astype(BF16)
        for part in range(2):
            sum_split[pl.ds(1024 * part + 256 * owner, 256), :] = result[
                :, LANES * part : LANES * (part + 1)
            ]
    begin(sum_split, land_split, 0, split_out)
    tick()

    def wide_up(part, chunk):
        def give(start, value):
            up_wide[
                pl.ds(start + chunk * half_rows, vsize), LANES * part : LANES * (part + 1)
            ] = value

        return give

    for chunk in range(2):
        for part in range(2):
            split_go.finish(2 * part + chunk, vsize, wide_up(part, chunk))
    split_go.drain()

    def keep_down(start, value):
        place = pl.ds(start + side, vsize)
        value = value.astype(BF16).astype(F32)
        moved = pltpu.roll(value * flags[place, 1:2], vsize - 1, 0)
        for half in range(2):
            lanes = slice(LANES * half, LANES * (half + 1))
            shifted[half, place, :] = value[:, lanes]
            shifted[2 + half, place, :] = moved[:, lanes]

    have("hat_down")
    norm_back(
        wide_ex[0],
        lambda place: up_wide[place, :],
        up_wide,
        hat_wide.at[0],
        gain_d[...],
        shift_d[...],
        inv_wide[0, 0:1, :],
        vec_wide.at[0],
        keep_down,
        tick,
    )

    def four_rows(start):
        place = pl.ds(start, vsize)
        here, below = pl.ds(start + side, vsize), pl.ds(start + 2 * side, vsize)
        keep = flags[below, 0:1]
        for kind in range(2):
            for half in range(2):
                lane = 256 * kind + LANES * half
                spread[place, lane : lane + LANES] = shifted[2 * kind + half, here, :].astype(BF16)
                spread[place, 512 + lane : 512 + lane + LANES] = (
                    shifted[2 * kind + half, below, :] * keep
                ).astype(BF16)

    tiles(rows, vsize, four_rows)
    have("features")

    def version(row_tap, col_tap):
        return 256 * (2 * (row_tap == 0) + (col_tap == 0))

    def phase_of(row_tap, col_tap):
        return 2 * (row_tap != 1) + (col_tap != 1)

    for row_tap in range(3):
        for col_tap in range(3):
            tap = 3 * row_tap + col_tap
            lane = version(row_tap, col_tap)
            for pair in range(2):
                phase = phase_of(row_tap, col_tap)
                left = join([fbuf[2 * pair + step, phase] for step in range(2)])
                sum_down[pl.ds(512 * tap + 256 * pair, 256), :] = lax.dot_general(
                    left, spread[:, lane : lane + 256], along_dims, preferred_element_type=F32
                ).astype(BF16)
        piece = pl.ds(1536 * row_tap, 1536)
        room = landing_rows(1536, batch_count)
        flat = dbuf.at[pl.ds(room * row_tap, room)]
        begin(sum_down.at[piece], flat, 1 if row_tap == 1 else 0, down_out.at[piece])
    have("down")

    down_go = Scatter(
        at,
        (
            lambda owner, phase: hbuf.at[phase, owner],
            lambda block, phase: jbuf.at[block, phase],
            lambda phase: rcross_d.at[phase],
            lambda phase: across_d.at[phase],
        ),
        send,
        recv,
        base[0],
    )
    order = (3, 2, 1, 0)

    def feature_terms(phase, pair):
        row_taps = (0, 2) if phase // 2 else (1,)
        col_taps = (0, 2) if phase % 2 else (1,)

        def body(start):
            place = pl.ds(start, msize)
            total = None
            for row_tap in row_taps:
                for col_tap in col_taps:
                    lane = version(row_tap, col_tap)
                    one = lax.dot_general(
                        spread[place, lane : lane + 256],
                        wd[3 * row_tap + col_tap, pair_rows(pair), :],
                        across_dims,
                        preferred_element_type=F32,
                    )
                    total = one if total is None else total + one
            terms = total.astype(BF16)
            for step in range(2):
                hbuf[phase, 2 * pair + step, place, :] = terms[:, LANES * step : LANES * (step + 1)]

        tiles(rows, msize, body)

    for phase in order:
        feature_terms(phase, 1 - at.pair)
        down_go.far_copy(phase).start()
    for phase in order:
        down_go.relay(phase, vsize)
        feature_terms(phase, at.pair)
        down_go.mate_copy(phase).start()
        tick(3)

    def place_back(phase):
        row_par, col_par = phase // 2, phase % 2

        def give(start, value):
            line = start // side
            for step in range(vsize // side):
                feat_grad[2 * (line + step) + row_par, pl.ds(col_par, side, stride=2), :] = value[
                    side * step : side * (step + 1), :
                ]

        return give

    for phase in order:
        down_go.finish(phase, vsize, place_back(phase))
        tick(3)
    down_go.drain()
    while queue:
        tick(len(queue))
    for made in (*wide_ex, *slim_ex):
        made.drain()


def backward_call(batch_count, side, grad_in, flags, weights, kept, inverses, vectors):
    rows = grad_in.shape[0]
    wide = 2 * LANES
    hbm = pl.BlockSpec(memory_space=pl.ANY)
    vmem = pl.BlockSpec(memory_space=pltpu.VMEM)
    dma = pltpu.SemaphoreType.DMA
    shape = jax.ShapeDtypeStruct
    bits = batch_count.bit_length() - 1
    near = list(range(bits))
    turned = [1, 0, *near[2:]] if bits > 1 else near
    feat_rows = 2 * rows // side * 1
    sums = [
        shape((1024, wide), BF16),
        shape((5120, LANES), BF16),
        shape((5120, LANES), BF16),
        shape((2560, LANES), BF16),
        shape((4608, wide), BF16),
    ]
    scratch = [
        pltpu.VMEM((rows, wide), BF16),
        pltpu.VMEM((9, 512, wide), BF16),
        pltpu.VMEM((1024, wide), BF16),
        pltpu.VMEM((2, 512, LANES), BF16),
        pltpu.VMEM((2, 512, 9 * LANES), BF16),
        pltpu.VMEM((512, LANES), BF16),
        pltpu.VMEM((1024, wide), BF16),
        pltpu.VMEM((4, 4, rows, LANES), BF16),
        pltpu.VMEM((4 * rows, wide), BF16),
        pltpu.VMEM((5, 4, rows, LANES), BF16),
        pltpu.VMEM((2, 4, rows, LANES), BF16),
        pltpu.VMEM((3, rows, wide), F32),
        pltpu.VMEM((5, rows, LANES), F32),
        pltpu.VMEM((rows, wide), F32),
        pltpu.VMEM((rows, LANES), F32),
        pltpu.VMEM((rows, LANES), F32),
        pltpu.VMEM((rows, LANES), F32),
        pltpu.VMEM((4, rows + 2 * side, LANES), F32),
        pltpu.VMEM((rows, 9 * LANES), BF16),
        pltpu.VMEM((rows, wide), BF16),
        pltpu.VMEM((rows, LANES), BF16),
        pltpu.VMEM((2, 4, rows, LANES), BF16),
        pltpu.VMEM((2, 2, 2, rows, LANES), BF16),
        pltpu.VMEM((2, 2, rows, LANES), BF16),
        pltpu.VMEM((2, rows, LANES), BF16),
        pltpu.VMEM((4, rows, LANES), BF16),
        pltpu.VMEM((4, rows, LANES), BF16),
        *[pltpu.VMEM(one.shape, one.dtype) for one in sums],
        *[
            pltpu.VMEM((landing_rows(one.shape[0], batch_count), one.shape[1]), one.dtype)
            for one in sums[:4]
        ],
        pltpu.VMEM((3, batch_count, 8, wide), F32),
        pltpu.VMEM((5, batch_count, 8, LANES), F32),
        dma((3, batch_count)),
        dma((5, batch_count)),
        dma((3, batch_count)),
        dma((5, batch_count)),
        dma((72,)),
        dma((72,)),
        dma((8 * 2 * bits,)),
        dma((8 * 2 * bits,)),
        dma((60,)),
        dma((12,)),
    ]
    return pl.pallas_call(
        functools.partial(backward_kernel, batch_count, side, (near, turned)),
        out_shape=[
            shape((feat_rows, 2 * side, LANES), F32),
            shape((3, 8, wide), F32),
            shape((5, 8, LANES), F32),
            *sums,
        ],
        in_specs=[hbm, vmem] + [hbm] * 6 + [hbm] * 6 + [vmem] * 2 + [vmem] * 10,
        out_specs=[vmem] * 3 + [hbm] * 5,
        scratch_shapes=scratch,
        compiler_params=pltpu.CompilerParams(
            collective_id=1, has_side_effects=True, vmem_limit_bytes=VMEM_LIMIT
        ),
    )(grad_in, flags, *weights, *kept, *inverses, *vectors)


def local(
    features,
    tile_split,
    out_grad,
    w_down,
    gain_down,
    shift_down,
    w_split,
    gain_split,
    shift_split,
    w_first,
    w_second,
    gain_block,
    shift_block,
    w_trans,
    gain_trans,
    shift_trans,
    w_merge,
    gain_merge,
    shift_merge,
):
    side = out_grad.shape[1]
    count = lax.axis_size("batch")
    flags = mask_columns(tile_split, side)

    def row(vec):
        return vec.reshape(1, -1)

    weights = (
        w_down.reshape(9, w_down.shape[2], w_down.shape[3]),
        w_split,
        w_first,
        w_second.reshape(2, 9, w_second.shape[3], w_second.shape[4]),
        w_trans,
        w_merge,
    )
    vectors = (
        row(gain_down),
        row(shift_down),
        gain_split,
        shift_split,
        gain_block.reshape(4, -1),
        shift_block.reshape(4, -1),
        row(gain_trans),
        row(shift_trans),
        row(gain_merge),
        row(shift_merge),
    )
    mixed, *kept = forward_call(
        count,
        side,
        features.reshape(-1, features.shape[2], features.shape[3]),
        flags,
        weights,
        vectors,
    )
    kept[1] = kept[1].reshape(-1, kept[1].shape[2])
    grad_rows = out_grad.reshape(-1, out_grad.shape[3])
    feat_grad, vec_wide, vec_slim, merge, late, early, split, down = backward_call(
        count, side, grad_rows, flags, weights, kept[:6], kept[6:], vectors
    )
    taps = w_second.shape[1:]
    nine = late.shape[0] - w_trans.shape[0]
    two = split.shape[0] - w_first.shape[1]
    second_grad = jnp.stack([early[:nine].reshape(taps), late[:nine].reshape(taps)])
    first_grad = jnp.stack([split[two:], early[nine:]])
    return (
        mixed.reshape(out_grad.shape),
        feat_grad.reshape(features.shape),
        down.reshape(w_down.shape).astype(F32),
        vec_wide[0, 1],
        vec_wide[0, 0],
        split[:two].reshape(w_split.shape).astype(F32),
        vec_wide[1, 1].reshape(gain_split.shape),
        vec_wide[1, 0].reshape(shift_split.shape),
        first_grad.astype(F32),
        second_grad.astype(F32),
        vec_slim[:4, 1].reshape(gain_block.shape),
        vec_slim[:4, 0].reshape(shift_block.shape),
        late[nine:].astype(F32),
        vec_slim[4, 1],
        vec_slim[4, 0],
        merge.astype(F32),
        vec_wide[2, 1],
        vec_wide[2, 0],
    )


def solution(mesh):
    placed = (
        P("batch", None, None, "chan"),
        P("batch", None),
        P("batch", None, None, "chan"),
        P(None, None, None, "chan"),
        P("chan"),
        P("chan"),
        P(None, None, "chan"),
        P(None, "chan"),
        P(None, "chan"),
        P(None, None, "chan"),
        P(None, None, None, None, "chan"),
        P(None, None, "chan"),
        P(None, None, "chan"),
        P(None, "chan"),
        P("chan"),
        P("chan"),
        P(None, "chan"),
        P("chan"),
        P("chan"),
    )
    return jax.shard_map(
        local,
        mesh=mesh,
        in_specs=placed,
        out_specs=(
            P("batch", None, None, "chan"),
            P("batch", None, None, "chan"),
            P(None, None, None, "chan"),
            P("chan"),
            P("chan"),
            P(None, None, "chan"),
            P(None, "chan"),
            P(None, "chan"),
            P(None, None, "chan"),
            P(None, None, None, None, "chan"),
            P(None, None, "chan"),
            P(None, None, "chan"),
            P(None, "chan"),
            P("chan"),
            P("chan"),
            P(None, "chan"),
            P("chan"),
            P("chan"),
        ),
        check_vma=False,
    )
```

profile of v0, /device:TPU:0, one launch (start us, length us, event | category | flops | bytes accessed | tf_op | source)
XLA Modules:
  0.0 463.2 jit_solution(9987405134181647043)
XLA Ops:
  0.8 1.0 slice_reduce_fusion
  2.1 0.1 stack_reshape.27
  2.2 0.1 stack_reshape.29
  2.5 0.1 stack_reshape.26
  2.8 0.1 stack_reshape.24
  2.9 0.2 copy.43
  3.2 0.9 pad.4.flags
  4.1 159.2 %shard_map.322 = (bf16[1152,256]{1,0:T(8,128)(2,1)}, bf16[4,4,1152,128]{3,2,1,0:T(8,128)(2,1)}, bf16[4,1152,256]{2,1,0:T(8,128)(2,1)}, bf16[5,4,1152,128]{3,2,1,...) custom-call(bf16[96,48,128]{2,1,0:T(8,128)(2,1)} %bitcast.60, ...), custom_call_target="tpu_custom_call" | custom-call | tf_op jit(solution)/shard_map/pallas_call | solution.py:717
  163.2 281.6 %shard_map.323 = (f32[96,48,128]{2,1,0:T(8,128)}, f32[3,8,256]{2,1,0:T(8,128)}, f32[5,8,128]{2,1,0:T(8,128)}, bf16[1024,256]{1,0:T(8,128)(2,1)}, bf16[5120,128]{...) custom-call(bf16[1152,256]{1,0:T(8,128)(2,1)} %bitcast.62, ...), custom_call_target="tpu_custom_call" | custom-call | tf_op jit(solution)/shard_map/pallas_call | solution.py:1613
  444.8 1.3 slice_bitcast_fusion.6
  446.1 1.4 fusion.3
  447.5 1.4 fusion.2
  448.9 1.0 slice_bitcast_fusion.1
  449.9 1.1 slice.86
  451.0 0.9 slice_bitcast_fusion
  452.0 0.8 maximum_convert_fusion.1
  452.8 0.7 slice_convert_fusion
  453.6 1.0 convert.7
  454.7 1.0 convert_element_type.43
  455.7 2.5 maximum_convert_fusion
  458.2 0.1 copy-done
  458.4 2.6 convert.6
  461.0 0.8 copy.46
  461.8 1.4 copy.47
  (33 shorter events, 1.0 us)
Async XLA Ops:
  444.8 7.1 %copy-start.3 = (bf16[5120,128]{1,0:T(8,128)(2,1)S(1)}, bf16[5120,128]{1,0:T(8,128)(2,1)}, u32[]{:S(2)}) copy-start(bf16[5120,128]{1,0:T(8,128)(2,1)} %get-tuple-element.48) | copy-start | bytes 3932164
  448.9 3.9 copy-start.2
  452.8 1.8 copy-start.5
  455.7 2.6 copy-start
  458.4 2.6 copy-start.4
  458.4 3.5 copy-start.1
where the time goes:
time: 466 us; the launch traced here: 463 us
  Pallas kernels  441 us (95%)
  local copies, waits for them, and re-layouts  12.5 us (3%)
  other arithmetic  9.15 us (2%)
    pallas_call x1, Pallas kernels, backward_call(): pl.pallas_call(functools.partial(backward_kernel, batch_count, side, (nea...  282 us
    pallas_call x1, Pallas kernels, forward_call(): pl.pallas_call(functools.partial(forward_kernel, batch_count, side), out_...  159 us

commit v1 on v0

--- a/solution.py
+++ b/solution.py
@@ -803,12 +803,33 @@
     return max(size for size in range(8, 321, 8) if rows % size == 0)
 
 
+class Links:
+    rate, latency = 50000.0, 2.5
+
+    def __init__(self):
+        self.free = {}
+
+    def plan(self, now, bit, size):
+        span = size / self.rate
+        loads = {2: ((1, span), (2, 2 * span))}.get(bit, ((bit, span),))
+        return {link: max(now, self.free.get(link, 0.0)) + load for link, load in loads}
+
+
 class Reducer:
     def __init__(self, places, buf, landing, out, order, sems, base, own_sem):
         self.at, self.buf, self.landing, self.out = places, buf, landing, out
         self.order, (self.send, self.recv), self.base = order, sems, base
         self.own_sem = own_sem
         self.low, self.size, self.taken, self.step = 0, buf.shape[0], 0, 0
+        self.due = 0.0
+
+    def next_load(self):
+        steps = len(self.order)
+        if self.step < steps:
+            bit, size = self.order[self.step], self.size // 2
+        else:
+            bit, size = self.order[2 * steps - 1 - self.step], self.size
+        return bit, 2 * size * self.buf.shape[1]
 
     def partner(self, bit):
         side = lax.rem(self.at.batch // (1 << bit), 2)
@@ -878,10 +899,15 @@
                 self.own.wait()
             self.low, self.size = self.next_low, 2 * self.size
         self.step += 1
-        if self.step == 2 * steps:
-            return True
-        self.launch()
-        return False
+        return self.step == 2 * steps
+
+
+first_row = (10240, 0)
+second_row = (512, 5120)
+trans_row = 9728
+split_row = 10752
+tap_ends = (2, 5, 7, 9)
+big_rows = 12800
 
 
 def landing_rows(rows, batch_count):
@@ -922,9 +948,7 @@
     vec_wide,
     vec_slim,
     merge_out,
-    late_out,
-    early_out,
-    split_out,
+    big_out,
     down_out,
     grad,
     wd,
@@ -954,14 +978,10 @@
     rcross_d,
     across_d,
     sum_merge,
-    sum_late,
-    sum_early,
-    sum_split,
+    sum_big,
     sum_down,
     land_merge,
-    land_late,
-    land_early,
-    land_split,
+    land_big,
     slots_wide,
     slots_slim,
     wide_sem,
@@ -1062,9 +1082,11 @@
     steps = 2 * len(orders[0])
     bbase = [0]
 
-    queue = []
-
-    def begin(buf, landing, order, out):
+    queue, held = [], []
+    links = Links()
+    quiet = [(start + 0.5, start + 6) for start in (30, 41, 59, 75, 93, 108, 130)]
+
+    def begin(buf, landing, order, out, now):
         made = Reducer(
             at,
             buf,
@@ -1076,20 +1098,50 @@
             osem.at[bbase[0] // steps],
         )
         bbase[0] += steps
-        made.launch()
-        queue.append(made)
-
-    def tick(most=1):
-        for made in list(queue)[:most]:
-            if made.advance():
-                queue.remove(made)
+        held.append(made)
+        resume(now)
+
+    def resume(now):
+        for made in list(held):
+            plan = links.plan(now, *made.next_load())
+            over = max(plan.values())
+            if any(now < end and over > start for start, end in quiet):
+                continue
+            links.free.update(plan)
+            made.due = over + links.latency
+            made.launch()
+            held.remove(made)
+            queue.append(made)
+
+    def step_on(made, now):
+        queue.remove(made)
+        if not made.advance():
+            held.append(made)
+            resume(now)
+
+    def pause(now):
+        while queue:
+            made = min(queue, key=lambda one: one.due)
+            if made.due > now:
+                break
+            step_on(made, now)
+        resume(now)
+
+    big_taken = [0]
+
+    def begin_rows(low, size, order, now):
+        room = landing_rows(size, batch_count)
+        where = pl.ds(low, size)
+        landing = land_big.at[pl.ds(big_taken[0], room)]
+        begin(sum_big.at[where], landing, order, big_out.at[where], now)
+        big_taken[0] += room
 
     at.greet()
 
     for ref in (shifted,):
         ref[...] = jnp.zeros_like(ref)
 
-    def norm_back(exchange, load, back, hat, gain, shift, inverse, vec_ref, give, meanwhile):
+    def norm_back(exchange, load, back, hat, gain, shift, inverse, vec_ref, give, now):
         width = back.shape[1]
 
         def first(index, carry):
@@ -1108,8 +1160,9 @@
         exchange.push(
             two_rows(jnp.sum(one, axis=0, keepdims=True), jnp.sum(two, axis=0, keepdims=True))
         )
-        meanwhile()
+        pause(now + 2)
         exchange.take()
+        pause(now + 6)
         slots = exchange.slots
 
         def gather_up(index, total):
@@ -1145,13 +1198,15 @@
     def pair_rows(pair, offset=0):
         return pl.ds(pl.multiple_of(offset + pair * 256, 256), 256)
 
-    def spread_out(go, left, weight_at, parts):
+    def spread_out(go, left, weight_at, parts, now, span):
         chunks = 2 * parts
         for chunk in range(chunks):
             back_pair(left, weight_at(chunk // 2, 1 - at.pair), 1 - at.pair, chunk % 2, chunk // 2)
             go.far_copy(chunk).start()
+        pause(now + 0.45 * span)
         for chunk in range(chunks):
             go.relay(chunk, vsize)
+        pause(now + 0.5 * span)
         for chunk in range(chunks):
             back_pair(left, weight_at(chunk // 2, at.pair), at.pair, chunk % 2, chunk // 2)
             go.mate_copy(chunk).start()
@@ -1175,7 +1230,7 @@
         inv_wide[2, 0:1, :],
         vec_wide.at[2],
         keep_wide,
-        lambda: None,
+        6,
     )
     have("merge")
     spread_out(
@@ -1183,6 +1238,8 @@
         lambda place: dz_wide[place, :],
         lambda part, pair: wm[pair_rows(pair, 512 * part), :],
         2,
+        12,
+        18,
     )
     have("joined")
     for part in range(2):
@@ -1190,7 +1247,7 @@
             sum_merge[pl.ds(512 * part + 256 * pair, 256), :] = lax.dot_general(
                 two_of(jbuf.at[part], pair), dz_wide[...], along_dims, preferred_element_type=F32
             ).astype(BF16)
-    begin(sum_merge, land_merge, 0, merge_out)
+    begin(sum_merge, land_merge, 0, merge_out, 24)
 
     def top_up(chunk):
         def give(start, value):
@@ -1204,7 +1261,7 @@
     def keep_slim(start, value):
         dz_slim[pl.ds(start, vsize), :] = value.astype(BF16)
 
-    def slim_back(index, load, gain, shift, give):
+    def slim_back(index, load, gain, shift, give, now):
         have(f"hat{index}")
         norm_back(
             slim_ex[index],
@@ -1216,10 +1273,16 @@
             inv_slim[index, 0:1, :],
             vec_slim.at[index],
             give,
-            tick,
-        )
-
-    def thin_back(stage, index, weight, name, target, offset, settle, extra=None):
+            now,
+        )
+
+    def settle_with(go, settle, now, span):
+        pause(now + 0.7 * span)
+        for chunk in range(2):
+            go.finish(chunk, vsize, settle(chunk))
+            pause(now + (0.85 + 0.15 * chunk) * span)
+
+    def thin_back(stage, index, weight, name, offset, settle, now, span):
         go = scatter(stage, 1)
         have(name)
         spread_out(
@@ -1227,20 +1290,18 @@
             lambda place: dz_slim[place, :],
             lambda part, pair: weight[pair_rows(pair), :],
             1,
+            now,
+            span,
         )
         have(f"half{index}")
         for pair in range(2):
-            target[pl.ds(offset + 256 * pair, 256), :] = lax.dot_general(
+            sum_big[pl.ds(offset + 256 * pair, 256), :] = lax.dot_general(
                 two_of(hbuf.at[index], pair), dz_slim[...], along_dims, preferred_element_type=F32
             ).astype(BF16)
-        if extra is not None:
-            extra()
-        tick()
-        for chunk in range(2):
-            go.finish(chunk, vsize, settle(chunk))
+        settle_with(go, settle, now, span)
         return go
 
-    slim_back(4, lambda place: up_slim[place, :], gain_t[...], shift_t[...], keep_slim)
+    slim_back(4, lambda place: up_slim[place, :], gain_t[...], shift_t[...], keep_slim, 30)
 
     def branch_new(chunk):
         def give(start, value):
@@ -1266,7 +1327,7 @@
         merge_go.drain()
 
     finish_bypass()
-    thin_back(1, 4, wt, "trans", sum_late, 4608, branch_new).drain()
+    thin_back(1, 4, wt, "trans", trans_row, branch_new, 30, 11).drain()
 
     def nine(start, value):
         place = pl.ds(start + side, vsize)
@@ -1286,7 +1347,7 @@
                     value = value * flags[source, column : column + 1]
                 spread[pl.ds(start, vsize), LANES * tap : LANES * (tap + 1)] = value.astype(BF16)
 
-    def tap_back(stage, layer, target, settle, extra):
+    def tap_back(stage, layer, offset, settle, begin_sums, now, span):
         index = 2 * layer + 1
         go = scatter(stage, 1)
         tiles(rows, vsize, nine_rows)
@@ -1296,6 +1357,8 @@
             lambda place: spread[place, :],
             lambda part, pair: w2[layer, pair_rows(pair), :],
             1,
+            now,
+            span,
         )
         have(f"half{index}")
         for pair in range(2):
@@ -1308,45 +1371,60 @@
                     preferred_element_type=F32,
                 ).astype(BF16)
                 for col_tap in range(3):
-                    target[pl.ds(512 * (3 * row_tap + col_tap) + 256 * pair, 256), :] = three[
+                    row = offset + 512 * (3 * row_tap + col_tap) + 256 * pair
+                    sum_big[pl.ds(row, 256), :] = three[
                         :, LANES * col_tap : LANES * (col_tap + 1)
                     ]
-        extra()
-        tick()
-        for chunk in range(2):
-            go.finish(chunk, vsize, settle(chunk))
+        begin_sums(now + 0.7 * span)
+        settle_with(go, settle, now, span)
         go.drain()
+
+    def late_sums(now):
+        begin_rows(second_row[1], 2560, 0, now)
+        begin_rows(second_row[1] + 2560, 2560, 1, now)
+
+    def early_sums(now):
+        begin_rows(0, 2560, 0, now)
+        begin_rows(2560, 2560, 1, now)
 
     for layer in (1, 0):
         stage = 2 if layer == 1 else 4
-        target = sum_late if layer == 1 else sum_early
+        now = 41 if layer == 1 else 75
         slim_back(
             2 * layer + 1,
             lambda place: branch[place, :],
             gain_b[2 * layer + 1 : 2 * layer + 2, :],
             shift_b[2 * layer + 1 : 2 * layer + 2, :],
             nine,
-        )
-        if layer == 1:
-            extra = lambda: begin(sum_late, land_late, 1, late_out)
-        else:
-            extra = lambda: begin(sum_early, land_early, 1, early_out)
-        tap_back(stage, layer, target, top_up, extra)
+            now,
+        )
+        tap_back(
+            stage,
+            layer,
+            second_row[layer],
+            top_up,
+            late_sums if layer == 1 else early_sums,
+            now,
+            18,
+        )
+        now += 18
         slim_back(
             2 * layer,
             lambda place: up_slim[place, :],
             gain_b[2 * layer : 2 * layer + 1, :],
             shift_b[2 * layer : 2 * layer + 1, :],
             keep_slim,
+            now,
         )
         thin_back(
             stage + 1,
             2 * layer,
             wf.at[layer],
             f"first{layer}",
-            sum_early if layer == 1 else sum_split,
-            4608 if layer == 1 else 2048,
+            first_row[layer],
             branch_more,
+            now,
+            15,
         ).drain()
 
     have("hat_split")
@@ -1360,7 +1438,7 @@
         inv_wide[1, 0:1, :],
         vec_wide.at[1],
         keep_wide,
-        tick,
+        108,
     )
     have("split")
     split_go = scatter(6, 2)
@@ -1383,10 +1461,12 @@
         split_terms(at.far, chunk)
         for part in range(2):
             split_go.far_copy(2 * part + chunk).start()
+    pause(115)
     for chunk in range(2):
         split_terms(at.cross, chunk)
         for part in range(2):
             split_go.relay(2 * part + chunk, vsize)
+    pause(118)
     for chunk in range(2):
         split_terms(at.mate, chunk)
         for part in range(2):
@@ -1399,11 +1479,11 @@
             dbuf[rows * owner : rows * (owner + 1), :], dz_wide[...], along_dims, preferred_element_type=F32
         ).astype(BF16)
         for part in range(2):
-            sum_split[pl.ds(1024 * part + 256 * owner, 256), :] = result[
+            sum_big[pl.ds(split_row + 1024 * part + 256 * owner, 256), :] = result[
                 :, LANES * part : LANES * (part + 1)
             ]
-    begin(sum_split, land_split, 0, split_out)
-    tick()
+    begin_rows(first_row[0], 2560, 0, 122)
+    pause(122)
 
     def wide_up(part, chunk):
         def give(start, value):
@@ -1416,6 +1496,7 @@
     for chunk in range(2):
         for part in range(2):
             split_go.finish(2 * part + chunk, vsize, wide_up(part, chunk))
+            pause(124 + 4 * chunk + 2 * part)
     split_go.drain()
 
     def keep_down(start, value):
@@ -1438,7 +1519,7 @@
         inv_wide[0, 0:1, :],
         vec_wide.at[0],
         keep_down,
-        tick,
+        130,
     )
 
     def four_rows(start):
@@ -1462,20 +1543,27 @@
     def phase_of(row_tap, col_tap):
         return 2 * (row_tap != 1) + (col_tap != 1)
 
-    for row_tap in range(3):
-        for col_tap in range(3):
-            tap = 3 * row_tap + col_tap
-            lane = version(row_tap, col_tap)
-            for pair in range(2):
-                phase = phase_of(row_tap, col_tap)
-                left = join([fbuf[2 * pair + step, phase] for step in range(2)])
-                sum_down[pl.ds(512 * tap + 256 * pair, 256), :] = lax.dot_general(
-                    left, spread[:, lane : lane + 256], along_dims, preferred_element_type=F32
-                ).astype(BF16)
-        piece = pl.ds(1536 * row_tap, 1536)
-        room = landing_rows(1536, batch_count)
-        flat = dbuf.at[pl.ds(room * row_tap, room)]
-        begin(sum_down.at[piece], flat, 1 if row_tap == 1 else 0, down_out.at[piece])
+    now = 137.0
+    taken = 0
+    for tap in range(9):
+        row_tap, col_tap = tap // 3, tap % 3
+        lane = version(row_tap, col_tap)
+        phase = phase_of(row_tap, col_tap)
+        for pair in range(2):
+            left = join([fbuf[2 * pair + step, phase] for step in range(2)])
+            sum_down[pl.ds(512 * tap + 256 * pair, 256), :] = lax.dot_general(
+                left, spread[:, lane : lane + 256], along_dims, preferred_element_type=F32
+            ).astype(BF16)
+        now += 0.5
+        if tap + 1 in tap_ends:
+            low = 512 * (([0, *tap_ends])[tap_ends.index(tap + 1)])
+            size = 512 * (tap + 1) - low
+            piece = pl.ds(low, size)
+            room = landing_rows(size, batch_count)
+            turn = tap_ends.index(tap + 1) % 3 == 1
+            begin(sum_down.at[piece], dbuf.at[pl.ds(taken, room)], int(turn), down_out.at[piece], now)
+            taken += room
+            pause(now)
     have("down")
 
     down_go = Scatter(
@@ -1518,11 +1606,14 @@
     for phase in order:
         feature_terms(phase, 1 - at.pair)
         down_go.far_copy(phase).start()
+        now += 1.5
+        pause(now)
     for phase in order:
         down_go.relay(phase, vsize)
         feature_terms(phase, at.pair)
         down_go.mate_copy(phase).start()
-        tick(3)
+        now += 1.7
+        pause(now)
 
     def place_back(phase):
         row_par, col_par = phase // 2, phase % 2
@@ -1536,12 +1627,18 @@
 
         return give
 
-    for phase in order:
-        down_go.finish(phase, vsize, place_back(phase))
-        tick(3)
+    arriving = [(147 + 5.9 * turn + 8.5, phase) for turn, phase in enumerate(order)]
+    while queue or held or arriving:
+        resume(now)
+        made = min(queue, key=lambda one: one.due) if queue else None
+        if arriving and (made is None or arriving[0][0] <= made.due):
+            due, phase = arriving.pop(0)
+            now = max(now, due)
+            down_go.finish(phase, vsize, place_back(phase))
+        else:
+            now = max(now, made.due)
+            step_on(made, now)
     down_go.drain()
-    while queue:
-        tick(len(queue))
     for made in (*wide_ex, *slim_ex):
         made.drain()
 
@@ -1556,12 +1653,10 @@
     bits = batch_count.bit_length() - 1
     near = list(range(bits))
     turned = [1, 0, *near[2:]] if bits > 1 else near
-    feat_rows = 2 * rows // side * 1
+    feat_rows = 2 * rows // side
     sums = [
         shape((1024, wide), BF16),
-        shape((5120, LANES), BF16),
-        shape((5120, LANES), BF16),
-        shape((2560, LANES), BF16),
+        shape((big_rows, LANES), BF16),
         shape((4608, wide), BF16),
     ]
     scratch = [
@@ -1595,7 +1690,7 @@
         *[pltpu.VMEM(one.shape, one.dtype) for one in sums],
         *[
             pltpu.VMEM((landing_rows(one.shape[0], batch_count), one.shape[1]), one.dtype)
-            for one in sums[:4]
+            for one in sums[:2]
         ],
         pltpu.VMEM((3, batch_count, 8, wide), F32),
         pltpu.VMEM((5, batch_count, 8, LANES), F32),
@@ -1605,10 +1700,10 @@
         dma((5, batch_count)),
         dma((72,)),
         dma((72,)),
-        dma((8 * 2 * bits,)),
-        dma((8 * 2 * bits,)),
+        dma((15 * 2 * bits,)),
+        dma((15 * 2 * bits,)),
         dma((60,)),
-        dma((12,)),
+        dma((15,)),
     ]
     return pl.pallas_call(
         functools.partial(backward_kernel, batch_count, side, (near, turned)),
@@ -1619,7 +1714,7 @@
             *sums,
         ],
         in_specs=[hbm, vmem] + [hbm] * 6 + [hbm] * 6 + [vmem] * 2 + [vmem] * 10,
-        out_specs=[vmem] * 3 + [hbm] * 5,
+        out_specs=[vmem] * 3 + [hbm] * 3,
         scratch_shapes=scratch,
         compiler_params=pltpu.CompilerParams(
             collective_id=1, has_side_effects=True, vmem_limit_bytes=VMEM_LIMIT
@@ -1685,28 +1780,27 @@
     )
     kept[1] = kept[1].reshape(-1, kept[1].shape[2])
     grad_rows = out_grad.reshape(-1, out_grad.shape[3])
-    feat_grad, vec_wide, vec_slim, merge, late, early, split, down = backward_call(
+    feat_grad, vec_wide, vec_slim, merge, big, down = backward_call(
         count, side, grad_rows, flags, weights, kept[:6], kept[6:], vectors
     )
-    taps = w_second.shape[1:]
-    nine = late.shape[0] - w_trans.shape[0]
-    two = split.shape[0] - w_first.shape[1]
-    second_grad = jnp.stack([early[:nine].reshape(taps), late[:nine].reshape(taps)])
-    first_grad = jnp.stack([split[two:], early[nine:]])
+    rows = w_trans.shape[0]
+    two = second_row[0]
+    second_grad = big[two : two + 18 * rows].reshape(w_second.shape)
+    first_grad = jnp.stack([big[low : low + rows] for low in first_row])
     return (
         mixed.reshape(out_grad.shape),
         feat_grad.reshape(features.shape),
         down.reshape(w_down.shape).astype(F32),
         vec_wide[0, 1],
         vec_wide[0, 0],
-        split[:two].reshape(w_split.shape).astype(F32),
+        big[split_row:].reshape(w_split.shape).astype(F32),
         vec_wide[1, 1].reshape(gain_split.shape),
         vec_wide[1, 0].reshape(shift_split.shape),
         first_grad.astype(F32),
         second_grad.astype(F32),
         vec_slim[:4, 1].reshape(gain_block.shape),
         vec_slim[:4, 0].reshape(shift_block.shape),
-        late[nine:].astype(F32),
+        big[trans_row : trans_row + rows].astype(F32),
         vec_slim[4, 1],
         vec_slim[4, 0],
         merge.astype(F32),

time: 466 us -> 407 us (0.87)
  Pallas kernels: 441 us -> 385 us
    pallas_call x1, Pallas kernels: 282 us -> 226 us  [backward_call(): pl.pallas_call(functools.partial(backward_kernel, batch_count, side, (nea...]
where the time goes in v1:
time: 407 us
  Pallas kernels  385 us (95%)
  local copies, waits for them, and re-layouts  10.5 us (3%)
  other arithmetic  10.4 us (3%)
    pallas_call x1, Pallas kernels, backward_call(): pl.pallas_call(functools.partial(backward_kernel, batch_count, side, (nea...  226 us
    pallas_call x1, Pallas kernels, forward_call(): pl.pallas_call(functools.partial(forward_kernel, batch_count, side), out_...  159 us

profile of v1, /device:TPU:0, one launch (start us, length us, event | category | flops | bytes accessed | tf_op | source)
XLA Modules:
  0.0 406.7 jit_solution(6443808676504834243)
XLA Ops:
  0.8 1.0 slice_reduce_fusion
  2.1 0.1 stack_reshape.21
  2.2 0.1 stack_reshape.23
  2.3 0.1 stack_reshape.19
  2.5 0.1 stack_reshape.20
  2.6 0.1 stack_reshape.22
  2.8 0.1 stack_reshape.18
  2.9 0.2 copy.43
  3.2 0.9 pad.4.flags
  4.1 159.2 %shard_map.322 = (bf16[1152,256]{1,0:T(8,128)(2,1)}, bf16[4,4,1152,128]{3,2,1,0:T(8,128)(2,1)}, bf16[4,1152,256]{2,1,0:T(8,128)(2,1)}, bf16[5,4,1152,128]{3,2,1,...) custom-call(bf16[96,48,128]{2,1,0:T(8,128)(2,1)} %bitcast.59, ...), custom_call_target="tpu_custom_call" | custom-call | tf_op jit(solution)/shard_map/pallas_call | solution.py:717
  163.2 225.9 %shard_map.323 = (f32[96,48,128]{2,1,0:T(8,128)}, f32[3,8,256]{2,1,0:T(8,128)}, f32[5,8,128]{2,1,0:T(8,128)}, bf16[1024,256]{1,0:T(8,128)(2,1)}, bf16[12800,128]{1,0:T(8,128)(2,1)}, /*index=5*/bf16[4608,256]{1,0:T(8,128)(2,1)}) custom-call(bf16[1152,256]{1,0:T(8,128)(2,1)} %bitcast.61, f32[1200,8]{1,0:T(8,128)} %pad.4.flags, bf16[9,512,256]{2,1,0:T(8,128)(2,1)} %bitcast.52, ...), custom_call_target="tpu_custom_call" | custom-call | tf_op jit(solution)/shard_map/pallas_call | solution.py:1708
  389.1 1.4 slice_bitcast_fusion.6
  390.5 1.4 fusion.3
  391.8 1.4 fusion.2
  393.2 1.1 slice.83
  394.3 1.0 convert.8
  395.3 1.8 slice_convert_fusion
  397.1 0.2 slice.88
  397.3 0.8 maximum_convert_fusion
  398.1 1.0 convert_element_type.47
  399.2 2.7 convert.9
  401.9 2.6 convert.7
  404.5 0.8 copy.46
  405.3 1.4 copy.47
  (28 shorter events, 0.7 us)
Async XLA Ops:
  389.1 8.0 %copy-start = (bf16[12800,128]{1,0:T(8,128)(2,1)S(1)}, bf16[12800,128]{1,0:T(8,128)(2,1)}, u32[]{:S(2)}) copy-start(bf16[12800,128]{1,0:T(8,128)(2,1)} %get-tuple-element.45) | copy-start | bytes 9830404
  397.1 1.0 copy-start.4
  399.2 2.7 copy-start.1
  401.9 2.6 copy-start.3
  401.9 3.5 copy-start.2

commit v2 on v1

--- a/solution.py
+++ b/solution.py
@@ -228,507 +228,6 @@
 
         variance = lax.fori_loop(0, count, squares, jnp.zeros((1, width), F32)) / self.pixels
         return whole, lax.rsqrt(variance + epsilon)
-
-
-def forward_kernel(
-    batch_count,
-    side,
-    feat,
-    flags,
-    wd_in,
-    ws_in,
-    wf_in,
-    w2_in,
-    wt_in,
-    wm_in,
-    gain_d,
-    shift_d,
-    gain_s,
-    shift_s,
-    gain_b,
-    shift_b,
-    gain_t,
-    shift_t,
-    gain_m,
-    shift_m,
-    mixed,
-    feat_out,
-    down_out,
-    half_out,
-    join_out,
-    wide_out,
-    slim_out,
-    inv_wide,
-    inv_slim,
-    wd,
-    ws,
-    wf,
-    w2,
-    wt,
-    wm,
-    raw,
-    fbuf,
-    dbuf,
-    hbuf,
-    jbuf,
-    hat_wide,
-    hat_slim,
-    acc_wide,
-    acc_slim,
-    z_wide,
-    z_slim,
-    branch,
-    slots_wide,
-    slots_slim,
-    wide_sem,
-    slim_sem,
-    wide_rsem,
-    slim_rsem,
-    send,
-    recv,
-    wsem,
-    osem,
-):
-    at = Places(batch_count)
-    me = at.chan
-    rows = z_wide.shape[0]
-    half_rows = rows // 2
-    pixels = rows * batch_count
-    area = side * side
-
-    weight_copies = {}
-
-    def bring(name, pairs):
-        copies = []
-        for source, target in pairs:
-            slot = sum(len(done) for done in weight_copies.values()) + len(copies)
-            copies.append(pltpu.make_async_copy(source, target, wsem.at[slot]))
-        weight_copies[name] = copies
-        for copy in copies:
-            copy.start()
-
-    def have(name):
-        for copy in weight_copies[name]:
-            copy.wait()
-
-    bring("down", [(wd_in.at[tap], wd.at[tap]) for tap in range(9)])
-    bring("split", [(ws_in.at[part], ws.at[:, pl.ds(LANES * part, LANES)]) for part in range(2)])
-    for layer in range(2):
-        bring(f"first{layer}", [(wf_in.at[layer], wf.at[layer])])
-        bring(
-            f"second{layer}",
-            [
-                (w2_in.at[layer, tap], w2.at[layer, :, pl.ds(LANES * tap, LANES)])
-                for tap in range(9)
-            ],
-        )
-    bring("trans", [(wt_in, wt)])
-    bring("merge", [(wm_in, wm)])
-
-    saved = []
-
-    def save(source, target):
-        copy = pltpu.make_async_copy(source, target, osem.at[len(saved)])
-        copy.start()
-        saved.append(copy)
-
-    base = [0]
-
-    def gather(view, chunks):
-        made = Gather(at, view, chunks, send, recv, base[0])
-        base[0] += 3 * chunks
-        return made
-
-    def by_half(ref):
-        return lambda owner, chunk: ref.at[owner, pl.ds(chunk * half_rows, half_rows)]
-
-    feat_go = gather(lambda owner, phase: fbuf.at[owner, phase], 4)
-    down_go = gather(by_half(dbuf), 2)
-    half_go = [gather(by_half(hbuf.at[index]), 2) for index in range(5)]
-    side_go = gather(by_half(jbuf.at[1]), 2)
-    top_go = gather(by_half(jbuf.at[0]), 2)
-    wide_ex = [
-        Exchange(at, slots_wide.at[index], wide_sem.at[index], wide_rsem.at[index])
-        for index in range(3)
-    ]
-    slim_ex = [
-        Exchange(at, slots_slim.at[index], slim_sem.at[index], slim_rsem.at[index])
-        for index in range(5)
-    ]
-
-    at.greet()
-
-    for phase in range(4):
-        row_par, col_par = phase // 2, phase % 2
-
-        if col_par == 0:
-
-            def widen(index, carry):
-                raw[index] = feat[2 * index + row_par].astype(F32)
-                return carry
-
-            lax.fori_loop(0, feat.shape[0] // 2, widen, 0)
-
-        def pick(start):
-            both = [
-                raw[2 * (start // (2 * side)) + step, pl.ds(col_par, side, stride=2), :]
-                for step in range(2)
-            ]
-            fbuf[me, phase, pl.ds(start, 2 * side), :] = jnp.concatenate(both, axis=0).astype(BF16)
-
-        tiles(rows, 2 * side, pick)
-        feat_go.start(phase)
-
-    acc_wide[...] = jnp.zeros_like(acc_wide)
-    have("down")
-
-    def down_pair(phase, pair):
-        row_par, col_par = phase // 2, phase % 2
-        row_taps = (0, 2) if row_par else (1,)
-        col_taps = (0, 2) if col_par else (1,)
-        size = 192
-
-        def body(start):
-            block = join(
-                [fbuf[2 * pair + step, phase, pl.ds(start, size), :] for step in range(2)]
-            )
-            for row_tap in row_taps:
-                for col_tap in col_taps:
-                    part = jnp.dot(
-                        block,
-                        wd[3 * row_tap + col_tap, pl.ds(pl.multiple_of(pair * 256, 256), 256), :],
-                        preferred_element_type=F32,
-                    )
-                    place = pl.ds(start + (2 * side if row_tap == 0 else side), size)
-                    if row_tap == 0:
-                        part = part * flags[place, 0:1]
-                    kind = 1 if col_tap == 0 else 0
-                    acc_wide[kind, place, :] += part
-
-        tiles(rows, size, body)
-
-    for phase in range(4):
-        feat_go.wait_mate(phase)
-        down_pair(phase, at.pair)
-        feat_go.forward(phase)
-    for phase in range(4):
-        feat_go.wait_far(phase)
-        down_pair(phase, 1 - at.pair)
-    save(fbuf, feat_out)
-
-    vsize = 4 * side
-
-    def settle_down(start):
-        place = pl.ds(start + side, vsize)
-        z_wide[pl.ds(start, vsize), :] = acc_wide[0, place, :] + flags[place, 1:2] * pltpu.roll(
-            acc_wide[1, place, :], 1, 0
-        )
-
-    tiles(rows, vsize, settle_down)
-
-    def activate(exchange, z_ref, hat_ref, gain, shift, inv_ref, give, begin):
-        mean, inverse = Norms(exchange, rows, pixels).statistics(z_ref)
-        inv_ref[...] = jnp.broadcast_to(inverse, inv_ref.shape)
-
-        def body(start):
-            place = pl.ds(start, vsize)
-            normed = (z_ref[place, :] - mean) * inverse
-            hat_ref[place, :] = normed
-            before = normed * gain + shift
-            _, top = mish_parts(before)
-            give(place, before * (top / (top + 2.0)))
-
-        for chunk in range(2):
-
-            def inner(start):
-                body(start + chunk * half_rows)
-
-            tiles(half_rows, vsize, inner)
-            begin(chunk)
-
-    def keep_down(place, value):
-        dbuf[me, place, :] = value.astype(BF16)
-
-    activate(
-        wide_ex[0], z_wide, hat_wide.at[0], gain_d[...], shift_d[...], inv_wide.at[0], keep_down,
-        down_go.start,
-    )
-    save(hat_wide.at[0], wide_out.at[0])
-    have("split")
-
-    msize = 192
-
-    def split_block(owner, chunk, first):
-        def body(start):
-            place = pl.ds(start + chunk * half_rows, msize)
-            part = jnp.dot(
-                dbuf[owner, place, :],
-                ws[pl.ds(pl.multiple_of(owner * 256, 256), 256), :],
-                preferred_element_type=F32,
-            )
-            if first:
-                z_wide[place, :] = part
-            else:
-                z_wide[place, :] += part
-
-        tiles(half_rows, msize, body)
-
-    for chunk in range(2):
-        split_block(me, chunk, True)
-    for chunk in range(2):
-        down_go.wait_mate(chunk)
-        split_block(at.mate, chunk, False)
-    for chunk in range(2):
-        down_go.forward(chunk)
-        split_block(at.cross, chunk, False)
-    for chunk in range(2):
-        down_go.wait_far(chunk)
-        split_block(at.far, chunk, False)
-    save(dbuf, down_out)
-
-    def keep_split(place, value):
-        branch[place, :] = value[:, :LANES]
-        hbuf[0, me, place, :] = value[:, :LANES].astype(BF16)
-        jbuf[1, me, place, :] = value[:, LANES:].astype(BF16)
-
-    activate(
-        wide_ex[1],
-        z_wide,
-        hat_wide.at[1],
-        join([gain_s[0:1, :], gain_s[1:2, :]]),
-        join([shift_s[0:1, :], shift_s[1:2, :]]),
-        inv_wide.at[1],
-        keep_split,
-        half_go[0].start,
-    )
-    save(hat_wide.at[1], wide_out.at[1])
-    for chunk in range(2):
-        side_go.start(chunk)
-
-    def two_of(ref, pair, place):
-        return join([ref[2 * pair + step, place, :] for step in range(2)])
-
-    def thin_pair(source, weight, pair, chunk, first):
-        def body(start):
-            place = pl.ds(start + chunk * half_rows, msize)
-            part = jnp.dot(
-                two_of(source, pair, place),
-                weight[pl.ds(pl.multiple_of(pair * 256, 256), 256), :],
-                preferred_element_type=F32,
-            )
-            if first:
-                z_slim[place, :] = part
-            else:
-                z_slim[place, :] += part
-
-        tiles(half_rows, msize, body)
-
-    def thin_conv(index, weight):
-        source, go = hbuf.at[index], half_go[index]
-        for chunk in range(2):
-            go.wait_mate(chunk)
-            thin_pair(source, weight, at.pair, chunk, True)
-        for chunk in range(2):
-            go.forward(chunk)
-        for chunk in range(2):
-            go.wait_far(chunk)
-            thin_pair(source, weight, 1 - at.pair, chunk, False)
-        save(source, half_out.at[index])
-
-    def tap_pair(source, weight, pair, chunk):
-        def body(start):
-            begin = start + chunk * half_rows
-            part = jnp.dot(
-                two_of(source, pair, pl.ds(begin, msize)),
-                weight[pl.ds(pl.multiple_of(pair * 256, 256), 256), :],
-                preferred_element_type=F32,
-            )
-            for col_tap in range(3):
-                for row_tap in range(3):
-                    tap = 3 * row_tap + col_tap
-                    piece = part[:, LANES * tap : LANES * (tap + 1)]
-                    place = pl.ds(begin + side - side * (row_tap - 1), msize)
-                    if row_tap != 1:
-                        column = 2 if row_tap == 0 else 3
-                        piece = piece * flags[place, column : column + 1]
-                    acc_slim[col_tap, place, :] += piece
-
-        tiles(half_rows, msize, body)
-
-    def tap_conv(index, weight):
-        source, go = hbuf.at[index], half_go[index]
-        acc_slim[...] = jnp.zeros_like(acc_slim)
-        for chunk in range(2):
-            go.wait_mate(chunk)
-            tap_pair(source, weight, at.pair, chunk)
-        for chunk in range(2):
-            go.forward(chunk)
-        for chunk in range(2):
-            go.wait_far(chunk)
-            tap_pair(source, weight, 1 - at.pair, chunk)
-        save(source, half_out.at[index])
-
-        def settle(start):
-            place = pl.ds(start + side, vsize)
-            z_slim[pl.ds(start, vsize), :] = (
-                acc_slim[1, place, :]
-                + flags[place, 4:5] * pltpu.roll(acc_slim[0, place, :], 1, 0)
-                + flags[place, 5:6] * pltpu.roll(acc_slim[2, place, :], vsize - 1, 0)
-            )
-
-        tiles(rows, vsize, settle)
-
-    def slim_act(index, gain, shift, give, begin):
-        activate(
-            slim_ex[index], z_slim, hat_slim.at[index], gain, shift, inv_slim.at[index], give, begin
-        )
-        save(hat_slim.at[index], slim_out.at[index])
-
-    for layer in range(2):
-        have(f"first{layer}")
-        thin_conv(2 * layer, wf.at[layer])
-
-        def keep_inner(place, value):
-            hbuf[2 * layer + 1, me, place, :] = value.astype(BF16)
-
-        slim_act(
-            2 * layer,
-            gain_b[2 * layer : 2 * layer + 1, :],
-            shift_b[2 * layer : 2 * layer + 1, :],
-            keep_inner,
-            half_go[2 * layer + 1].start,
-        )
-        have(f"second{layer}")
-        tap_conv(2 * layer + 1, w2.at[layer])
-
-        def keep_branch(place, value):
-            total = branch[place, :] + value
-            branch[place, :] = total
-            hbuf[2 * layer + 2, me, place, :] = total.astype(BF16)
-
-        slim_act(
-            2 * layer + 1,
-            gain_b[2 * layer + 1 : 2 * layer + 2, :],
-            shift_b[2 * layer + 1 : 2 * layer + 2, :],
-            keep_branch,
-            half_go[2 * layer + 2].start,
-        )
-        if layer == 0:
-            for chunk in range(2):
-                side_go.forward(chunk)
-    have("trans")
-    thin_conv(4, wt)
-
-    def keep_top(place, value):
-        jbuf[0, me, place, :] = value.astype(BF16)
-
-    slim_act(4, gain_t[...], shift_t[...], keep_top, top_go.start)
-    have("merge")
-
-    def merge_pair(part_index, pair, chunk, first):
-        def body(start):
-            place = pl.ds(start + chunk * half_rows, msize)
-            part = jnp.dot(
-                two_of(jbuf.at[part_index], pair, place),
-                wm[pl.ds(pl.multiple_of(part_index * 512 + pair * 256, 256), 256), :],
-                preferred_element_type=F32,
-            )
-            if first:
-                z_wide[place, :] = part
-            else:
-                z_wide[place, :] += part
-
-        tiles(half_rows, msize, body)
-
-    for chunk in range(2):
-        side_go.wait_mate(chunk)
-        merge_pair(1, at.pair, chunk, True)
-    for chunk in range(2):
-        side_go.wait_far(chunk)
-        merge_pair(1, 1 - at.pair, chunk, False)
-    for chunk in range(2):
-        top_go.wait_mate(chunk)
-        merge_pair(0, at.pair, chunk, False)
-    for chunk in range(2):
-        top_go.forward(chunk)
-    for chunk in range(2):
-        top_go.wait_far(chunk)
-        merge_pair(0, 1 - at.pair, chunk, False)
-    save(jbuf, join_out)
-
-    def keep_mixed(place, value):
-        mixed[place, :] = value.astype(BF16)
-
-    activate(
-        wide_ex[2], z_wide, hat_wide.at[2], gain_m[...], shift_m[...], inv_wide.at[2], keep_mixed,
-        lambda chunk: None,
-    )
-    save(hat_wide.at[2], wide_out.at[2])
-
-    for made in (feat_go, down_go, *half_go, side_go, top_go):
-        made.drain()
-    for made in (*wide_ex, *slim_ex):
-        made.drain()
-    for copy in saved:
-        copy.wait()
-
-
-def forward_call(batch_count, side, feat, flags, weights, vectors):
-    rows = feat.shape[0] * side // 2
-    wide = 2 * LANES
-    hbm = pl.BlockSpec(memory_space=pl.ANY)
-    vmem = pl.BlockSpec(memory_space=pltpu.VMEM)
-    dma = pltpu.SemaphoreType.DMA
-    shape = jax.ShapeDtypeStruct
-    kept = [
-        shape((4, 4, rows, LANES), BF16),
-        shape((4, rows, wide), BF16),
-        shape((5, 4, rows, LANES), BF16),
-        shape((2, 4, rows, LANES), BF16),
-        shape((3, rows, wide), F32),
-        shape((5, rows, LANES), F32),
-    ]
-    taps_width = 9 * LANES
-    scratch = [
-        pltpu.VMEM((9, 512, wide), BF16),
-        pltpu.VMEM((1024, wide), BF16),
-        pltpu.VMEM((2, 512, LANES), BF16),
-        pltpu.VMEM((2, 512, taps_width), BF16),
-        pltpu.VMEM((512, LANES), BF16),
-        pltpu.VMEM((1024, wide), BF16),
-        pltpu.VMEM((feat.shape[0] // 2, feat.shape[1], LANES), F32),
-        *[pltpu.VMEM(one.shape, one.dtype) for one in kept],
-        pltpu.VMEM((2, rows + 2 * side, wide), F32),
-        pltpu.VMEM((3, rows + 2 * side, LANES), F32),
-        pltpu.VMEM((rows, wide), F32),
-        pltpu.VMEM((rows, LANES), F32),
-        pltpu.VMEM((rows, LANES), F32),
-        pltpu.VMEM((3, batch_count, 8, wide), F32),
-        pltpu.VMEM((5, batch_count, 8, LANES), F32),
-        dma((3, batch_count)),
-        dma((5, batch_count)),
-        dma((3, batch_count)),
-        dma((5, batch_count)),
-        dma((60,)),
-        dma((60,)),
-        dma((40,)),
-        dma((20,)),
-    ]
-    return pl.pallas_call(
-        functools.partial(forward_kernel, batch_count, side),
-        out_shape=[
-            shape((rows, wide), BF16),
-            *kept,
-            shape((3, 8, wide), F32),
-            shape((5, 8, LANES), F32),
-        ],
-        in_specs=[vmem, vmem] + [hbm] * 6 + [vmem] * 10,
-        out_specs=[vmem] + [hbm] * 6 + [vmem, vmem],
-        scratch_shapes=scratch,
-        compiler_params=pltpu.CompilerParams(
-            collective_id=0, has_side_effects=True, vmem_limit_bytes=VMEM_LIMIT
-        ),
-    )(feat, flags, *weights, *vectors)
 
 
 class Scatter:
@@ -914,26 +413,11 @@
     return rows - rows // batch_count
 
 
-def backward_kernel(
+def section_kernel(
     batch_count,
     side,
     orders,
-    grad_in,
     flags,
-    wd_in,
-    ws_in,
-    wf_in,
-    w2_in,
-    wt_in,
-    wm_in,
-    feat_in,
-    down_in,
-    half_in,
-    join_in,
-    wide_in,
-    slim_in,
-    inv_wide,
-    inv_slim,
     gain_d,
     shift_d,
     gain_s,
@@ -944,12 +428,22 @@
     shift_t,
     gain_m,
     shift_m,
+    feat_in,
+    grad_in,
+    wd_in,
+    ws_in,
+    wf_in,
+    w2_in,
+    wt_in,
+    wm_in,
+    mixed,
     feat_grad,
     vec_wide,
     vec_slim,
     merge_out,
     big_out,
     down_out,
+    feat,
     grad,
     wd,
     ws,
@@ -963,11 +457,13 @@
     jbuf,
     hat_wide,
     hat_slim,
-    up_wide,
-    up_slim,
+    inv_wide,
+    inv_slim,
+    acc,
+    z_wide,
+    z_slim,
     branch,
     bypass,
-    shifted,
     spread,
     dz_wide,
     dz_slim,
@@ -976,11 +472,9 @@
     rcross,
     across,
     rcross_d,
-    across_d,
     sum_merge,
     sum_big,
     sum_down,
-    land_merge,
     land_big,
     slots_wide,
     slots_slim,
@@ -990,62 +484,72 @@
     slim_rsem,
     send,
     recv,
+    tsend,
+    trecv,
     bsend,
     brecv,
     wsem,
     osem,
 ):
+    raw = feat_grad
     at = Places(batch_count)
-    rows = up_wide.shape[0]
+    me = at.chan
+    rows = z_wide.shape[0]
     half_rows = rows // 2
     pixels = rows * batch_count
-    vsize = 4 * side
-    msize = 192
-
-    fetched = {}
-    count = [0]
-
-    def bring(name, *pairs):
+    area = side * side
+
+    weight_copies = {}
+
+    def bring(name, pairs):
         copies = []
         for source, target in pairs:
-            copies.append(pltpu.make_async_copy(source, target, wsem.at[count[0]]))
-            count[0] += 1
-        fetched[name] = copies
+            slot = sum(len(done) for done in weight_copies.values()) + len(copies)
+            copies.append(pltpu.make_async_copy(source, target, wsem.at[slot]))
+        weight_copies[name] = copies
         for copy in copies:
             copy.start()
 
     def have(name):
-        for copy in fetched[name]:
+        for copy in weight_copies[name]:
             copy.wait()
 
-    bring("grad", (grad_in, grad), (wide_in.at[2], hat_wide.at[2]))
-    bring("merge", (wm_in, wm))
-    bring("joined", (join_in, jbuf))
-    bring("hat4", (slim_in.at[4], hat_slim.at[4]))
-    bring("trans", (wt_in, wt))
-    bring("half4", (half_in.at[4], hbuf.at[4]))
-    for layer in (1, 0):
-        index = 2 * layer + 1
-        bring(f"hat{index}", (slim_in.at[index], hat_slim.at[index]))
+    bring("features", [(feat_in, feat)])
+    bring("down", [(wd_in.at[tap], wd.at[tap]) for tap in range(9)])
+    bring("split", [(ws_in.at[part], ws.at[:, pl.ds(LANES * part, LANES)]) for part in range(2)])
+    for layer in range(2):
+        bring(f"first{layer}", [(wf_in.at[layer], wf.at[layer])])
         bring(
             f"second{layer}",
-            *[
+            [
                 (w2_in.at[layer, tap], w2.at[layer, :, pl.ds(LANES * tap, LANES)])
                 for tap in range(9)
             ],
         )
-        bring(f"half{index}", (half_in.at[index], hbuf.at[index]))
-        index = 2 * layer
-        bring(f"hat{index}", (slim_in.at[index], hat_slim.at[index]))
-        bring(f"first{layer}", (wf_in.at[layer], wf.at[layer]))
-        bring(f"half{index}", (half_in.at[index], hbuf.at[index]))
-    bring("hat_split", (wide_in.at[1], hat_wide.at[1]))
-    bring("split", *[(ws_in.at[part], ws.at[:, pl.ds(LANES * part, LANES)]) for part in range(2)])
-    bring("down_low", (down_in, dbuf))
-    bring("hat_down", (wide_in.at[0], hat_wide.at[0]))
-    bring("features", (feat_in, fbuf))
-    bring("down", *[(wd_in.at[tap], wd.at[tap]) for tap in range(9)])
-
+    bring("trans", [(wt_in, wt)])
+    bring("merge", [(wm_in, wm)])
+    bring("grad", [(grad_in, grad)])
+
+    base = [0]
+
+    def gather(view, chunks):
+        made = Gather(at, view, chunks, send, recv, base[0])
+        base[0] += 3 * chunks
+        return made
+
+    def by_half(ref):
+        return lambda owner, chunk: ref.at[owner, pl.ds(chunk * half_rows, half_rows)]
+
+    feat_go = gather(lambda owner, phase: fbuf.at[owner, phase], 4)
+    def down_rows(owner, start, size):
+        return pl.ds(pl.multiple_of(owner * rows + start, 16), size)
+
+    down_go = gather(
+        lambda owner, chunk: dbuf.at[down_rows(owner, chunk * half_rows, half_rows)], 2
+    )
+    half_go = [gather(by_half(hbuf.at[index]), 2) for index in range(5)]
+    side_go = gather(by_half(jbuf.at[1]), 2)
+    top_go = gather(by_half(jbuf.at[0]), 2)
     wide_ex = [
         Exchange(at, slots_wide.at[index], wide_sem.at[index], wide_rsem.at[index])
         for index in range(3)
@@ -1055,6 +559,325 @@
         for index in range(5)
     ]
 
+    at.greet()
+
+    have("features")
+
+    for phase in range(4):
+        row_par, col_par = phase // 2, phase % 2
+
+        if col_par == 0:
+
+            def widen(index, carry):
+                line = pl.multiple_of((2 * index + row_par) * 2 * side, 16)
+                raw[index] = feat[pl.ds(line, 2 * side), :].astype(F32)
+                return carry
+
+            lax.fori_loop(0, raw.shape[0] // 2, widen, 0)
+
+        def pick(start):
+            both = [
+                raw[2 * (start // (2 * side)) + step, pl.ds(col_par, side, stride=2), :]
+                for step in range(2)
+            ]
+            fbuf[me, phase, pl.ds(start, 2 * side), :] = jnp.concatenate(both, axis=0).astype(BF16)
+
+        tiles(rows, 2 * side, pick)
+        feat_go.start(phase)
+
+    acc[...] = jnp.zeros_like(acc)
+    have("down")
+
+    def down_pair(phase, pair):
+        row_par, col_par = phase // 2, phase % 2
+        row_taps = (0, 2) if row_par else (1,)
+        col_taps = (0, 2) if col_par else (1,)
+        size = 192
+
+        def body(start):
+            block = join(
+                [fbuf[2 * pair + step, phase, pl.ds(start, size), :] for step in range(2)]
+            )
+            for row_tap in row_taps:
+                for col_tap in col_taps:
+                    part = jnp.dot(
+                        block,
+                        wd[3 * row_tap + col_tap, pl.ds(pl.multiple_of(pair * 256, 256), 256), :],
+                        preferred_element_type=F32,
+                    )
+                    place = pl.ds(start + (2 * side if row_tap == 0 else side), size)
+                    if row_tap == 0:
+                        part = part * flags[place, 0:1]
+                    kind = 1 if col_tap == 0 else 0
+                    for half in range(2):
+                        acc[2 * kind + half, place, :] += part[:, LANES * half : LANES * (half + 1)]
+
+        tiles(rows, size, body)
+
+    for phase in range(4):
+        feat_go.wait_mate(phase)
+        down_pair(phase, at.pair)
+        feat_go.forward(phase)
+    for phase in range(4):
+        feat_go.wait_far(phase)
+        down_pair(phase, 1 - at.pair)
+
+    vsize = 4 * side
+
+    def settle_down(start):
+        place = pl.ds(start + side, vsize)
+        for half in range(2):
+            z_wide[pl.ds(start, vsize), LANES * half : LANES * (half + 1)] = acc[
+                half, place, :
+            ] + flags[place, 1:2] * pltpu.roll(acc[2 + half, place, :], 1, 0)
+
+    tiles(rows, vsize, settle_down)
+
+    def activate(exchange, z_ref, hat_ref, gain, shift, inv_ref, give, begin):
+        mean, inverse = Norms(exchange, rows, pixels).statistics(z_ref)
+        inv_ref[...] = jnp.broadcast_to(inverse, inv_ref.shape)
+
+        def body(start):
+            place = pl.ds(start, vsize)
+            normed = (z_ref[place, :] - mean) * inverse
+            hat_ref[place, :] = normed
+            before = normed * gain + shift
+            _, top = mish_parts(before)
+            give(start, before * (top / (top + 2.0)))
+
+        for chunk in range(2):
+
+            def inner(start):
+                body(start + chunk * half_rows)
+
+            tiles(half_rows, vsize, inner)
+            begin(chunk)
+
+    def keep_down(start, value):
+        dbuf[down_rows(me, start, vsize), :] = value.astype(BF16)
+
+    activate(
+        wide_ex[0], z_wide, hat_wide.at[0], gain_d[...], shift_d[...], inv_wide.at[0], keep_down,
+        down_go.start,
+    )
+    have("split")
+
+    msize = 192
+
+    def split_block(owner, chunk, first):
+        def body(start):
+            place = pl.ds(start + chunk * half_rows, msize)
+            part = jnp.dot(
+                dbuf[down_rows(owner, start + chunk * half_rows, msize), :],
+                ws[pl.ds(pl.multiple_of(owner * 256, 256), 256), :],
+                preferred_element_type=F32,
+            )
+            if first:
+                z_wide[place, :] = part
+            else:
+                z_wide[place, :] += part
+
+        tiles(half_rows, msize, body)
+
+    for chunk in range(2):
+        split_block(me, chunk, True)
+    for chunk in range(2):
+        down_go.wait_mate(chunk)
+        split_block(at.mate, chunk, False)
+    for chunk in range(2):
+        down_go.forward(chunk)
+        split_block(at.cross, chunk, False)
+    for chunk in range(2):
+        down_go.wait_far(chunk)
+        split_block(at.far, chunk, False)
+
+    def keep_split(start, value):
+        place = pl.ds(start, vsize)
+        branch[place, :] = value[:, :LANES]
+        hbuf[0, me, place, :] = value[:, :LANES].astype(BF16)
+        jbuf[1, me, place, :] = value[:, LANES:].astype(BF16)
+
+    activate(
+        wide_ex[1],
+        z_wide,
+        hat_wide.at[1],
+        join([gain_s[0:1, :], gain_s[1:2, :]]),
+        join([shift_s[0:1, :], shift_s[1:2, :]]),
+        inv_wide.at[1],
+        keep_split,
+        half_go[0].start,
+    )
+    for chunk in range(2):
+        side_go.start(chunk)
+
+    def two_of(ref, pair, place):
+        return join([ref[2 * pair + step, place, :] for step in range(2)])
+
+    def thin_pair(source, weight, pair, chunk, first):
+        def body(start):
+            place = pl.ds(start + chunk * half_rows, msize)
+            part = jnp.dot(
+                two_of(source, pair, place),
+                weight[pl.ds(pl.multiple_of(pair * 256, 256), 256), :],
+                preferred_element_type=F32,
+            )
+            if first:
+                z_slim[place, :] = part
+            else:
+                z_slim[place, :] += part
+
+        tiles(half_rows, msize, body)
+
+    def thin_conv(index, weight):
+        source, go = hbuf.at[index], half_go[index]
+        for chunk in range(2):
+            go.wait_mate(chunk)
+            thin_pair(source, weight, at.pair, chunk, True)
+        for chunk in range(2):
+            go.forward(chunk)
+        for chunk in range(2):
+            go.wait_far(chunk)
+            thin_pair(source, weight, 1 - at.pair, chunk, False)
+
+    def tap_pair(source, weight, pair, chunk):
+        def body(start):
+            begin = start + chunk * half_rows
+            part = jnp.dot(
+                two_of(source, pair, pl.ds(begin, msize)),
+                weight[pl.ds(pl.multiple_of(pair * 256, 256), 256), :],
+                preferred_element_type=F32,
+            )
+            for col_tap in range(3):
+                for row_tap in range(3):
+                    tap = 3 * row_tap + col_tap
+                    piece = part[:, LANES * tap : LANES * (tap + 1)]
+                    place = pl.ds(begin + side - side * (row_tap - 1), msize)
+                    if row_tap != 1:
+                        column = 2 if row_tap == 0 else 3
+                        piece = piece * flags[place, column : column + 1]
+                    acc[col_tap, place, :] += piece
+
+        tiles(half_rows, msize, body)
+
+    def tap_conv(index, weight):
+        source, go = hbuf.at[index], half_go[index]
+        acc[0:3] = jnp.zeros((3, *acc.shape[1:]), F32)
+        for chunk in range(2):
+            go.wait_mate(chunk)
+            tap_pair(source, weight, at.pair, chunk)
+        for chunk in range(2):
+            go.forward(chunk)
+        for chunk in range(2):
+            go.wait_far(chunk)
+            tap_pair(source, weight, 1 - at.pair, chunk)
+
+        def settle(start):
+            place = pl.ds(start + side, vsize)
+            z_slim[pl.ds(start, vsize), :] = (
+                acc[1, place, :]
+                + flags[place, 4:5] * pltpu.roll(acc[0, place, :], 1, 0)
+                + flags[place, 5:6] * pltpu.roll(acc[2, place, :], vsize - 1, 0)
+            )
+
+        tiles(rows, vsize, settle)
+
+    def slim_act(index, gain, shift, give, begin):
+        activate(
+            slim_ex[index], z_slim, hat_slim.at[index], gain, shift, inv_slim.at[index], give, begin
+        )
+
+    for layer in range(2):
+        have(f"first{layer}")
+        thin_conv(2 * layer, wf.at[layer])
+
+        def keep_inner(start, value):
+            place = pl.ds(start, vsize)
+            hbuf[2 * layer + 1, me, place, :] = value.astype(BF16)
+
+        slim_act(
+            2 * layer,
+            gain_b[2 * layer : 2 * layer + 1, :],
+            shift_b[2 * layer : 2 * layer + 1, :],
+            keep_inner,
+            half_go[2 * layer + 1].start,
+        )
+        have(f"second{layer}")
+        tap_conv(2 * layer + 1, w2.at[layer])
+
+        def keep_branch(start, value):
+            place = pl.ds(start, vsize)
+            total = branch[place, :] + value
+            branch[place, :] = total
+            hbuf[2 * layer + 2, me, place, :] = total.astype(BF16)
+
+        slim_act(
+            2 * layer + 1,
+            gain_b[2 * layer + 1 : 2 * layer + 2, :],
+            shift_b[2 * layer + 1 : 2 * layer + 2, :],
+            keep_branch,
+            half_go[2 * layer + 2].start,
+        )
+        if layer == 0:
+            for chunk in range(2):
+                side_go.forward(chunk)
+    have("trans")
+    thin_conv(4, wt)
+
+    def keep_top(start, value):
+        place = pl.ds(start, vsize)
+        jbuf[0, me, place, :] = value.astype(BF16)
+
+    slim_act(4, gain_t[...], shift_t[...], keep_top, top_go.start)
+    have("merge")
+
+    def merge_pair(part_index, pair, chunk, first):
+        def body(start):
+            place = pl.ds(start + chunk * half_rows, msize)
+            part = jnp.dot(
+                two_of(jbuf.at[part_index], pair, place),
+                wm[pl.ds(pl.multiple_of(part_index * 512 + pair * 256, 256), 256), :],
+                preferred_element_type=F32,
+            )
+            if first:
+                z_wide[place, :] = part
+            else:
+                z_wide[place, :] += part
+
+        tiles(half_rows, msize, body)
+
+    for chunk in range(2):
+        side_go.wait_mate(chunk)
+        merge_pair(1, at.pair, chunk, True)
+    for chunk in range(2):
+        side_go.wait_far(chunk)
+        merge_pair(1, 1 - at.pair, chunk, False)
+    for chunk in range(2):
+        top_go.wait_mate(chunk)
+        merge_pair(0, at.pair, chunk, False)
+    for chunk in range(2):
+        top_go.forward(chunk)
+    for chunk in range(2):
+        top_go.wait_far(chunk)
+        merge_pair(0, 1 - at.pair, chunk, False)
+
+    def keep_mixed(start, value):
+        place = pl.ds(start, vsize)
+        spread[place, 0:256] = value.astype(BF16)
+
+    activate(
+        wide_ex[2], z_wide, hat_wide.at[2], gain_m[...], shift_m[...], inv_wide.at[2], keep_mixed,
+        lambda chunk: None,
+    )
+
+    for made in (feat_go, down_go, *half_go, side_go, top_go):
+        made.drain()
+    for made in (*wide_ex, *slim_ex):
+        made.drain()
+    mixed_copy = pltpu.make_async_copy(spread.at[:, pl.ds(0, 256)], mixed, osem.at[15])
+    mixed_copy.start()
+
+    wide_ex = [wide_ex[index] for index in (2, 1, 0)]
+
     base = [0]
 
     def scatter(stage, parts):
@@ -1075,7 +898,7 @@
         def over(chunk):
             return cut(across)(chunk // 2, chunk % 2)
 
-        made = Scatter(at, (term, from_mate, from_cross, over), send, recv, base[0])
+        made = Scatter(at, (term, from_mate, from_cross, over), tsend, trecv, base[0])
         base[0] += 6 * parts
         return made
 
@@ -1136,10 +959,8 @@
         begin(sum_big.at[where], landing, order, big_out.at[where], now)
         big_taken[0] += room
 
-    at.greet()
-
-    for ref in (shifted,):
-        ref[...] = jnp.zeros_like(ref)
+    for low in (0, rows + side):
+        acc[:, low : low + side, :] = jnp.zeros((acc.shape[0], side, LANES), F32)
 
     def norm_back(exchange, load, back, hat, gain, shift, inverse, vec_ref, give, now):
         width = back.shape[1]
@@ -1223,7 +1044,7 @@
     norm_back(
         wide_ex[2],
         lambda place: grad[place, :].astype(F32),
-        up_wide,
+        z_wide,
         hat_wide.at[2],
         gain_m[...],
         shift_m[...],
@@ -1232,7 +1053,6 @@
         keep_wide,
         6,
     )
-    have("merge")
     spread_out(
         merge_go,
         lambda place: dz_wide[place, :],
@@ -1241,17 +1061,16 @@
         12,
         18,
     )
-    have("joined")
     for part in range(2):
         for pair in range(2):
             sum_merge[pl.ds(512 * part + 256 * pair, 256), :] = lax.dot_general(
                 two_of(jbuf.at[part], pair), dz_wide[...], along_dims, preferred_element_type=F32
             ).astype(BF16)
-    begin(sum_merge, land_merge, 0, merge_out, 24)
+    begin(sum_merge, grad.at[pl.ds(0, landing_rows(1024, batch_count))], 0, merge_out, 24)
 
     def top_up(chunk):
         def give(start, value):
-            up_slim[pl.ds(start + chunk * half_rows, vsize), :] = value
+            z_slim[pl.ds(start + chunk * half_rows, vsize), :] = value
 
         return give
 
@@ -1262,11 +1081,10 @@
         dz_slim[pl.ds(start, vsize), :] = value.astype(BF16)
 
     def slim_back(index, load, gain, shift, give, now):
-        have(f"hat{index}")
         norm_back(
             slim_ex[index],
             load,
-            up_slim,
+            z_slim,
             hat_slim.at[index],
             gain,
             shift,
@@ -1282,9 +1100,8 @@
             go.finish(chunk, vsize, settle(chunk))
             pause(now + (0.85 + 0.15 * chunk) * span)
 
-    def thin_back(stage, index, weight, name, offset, settle, now, span):
+    def thin_back(stage, index, weight, offset, settle, now, span):
         go = scatter(stage, 1)
-        have(name)
         spread_out(
             go,
             lambda place: dz_slim[place, :],
@@ -1293,7 +1110,6 @@
             now,
             span,
         )
-        have(f"half{index}")
         for pair in range(2):
             sum_big[pl.ds(offset + 256 * pair, 256), :] = lax.dot_general(
                 two_of(hbuf.at[index], pair), dz_slim[...], along_dims, preferred_element_type=F32
@@ -1301,7 +1117,7 @@
         settle_with(go, settle, now, span)
         return go
 
-    slim_back(4, lambda place: up_slim[place, :], gain_t[...], shift_t[...], keep_slim, 30)
+    slim_back(4, lambda place: z_slim[place, :], gain_t[...], shift_t[...], keep_slim, 30)
 
     def branch_new(chunk):
         def give(start, value):
@@ -1327,21 +1143,21 @@
         merge_go.drain()
 
     finish_bypass()
-    thin_back(1, 4, wt, "trans", trans_row, branch_new, 30, 11).drain()
+    thin_back(1, 4, wt, trans_row, branch_new, 30, 11).drain()
 
     def nine(start, value):
         place = pl.ds(start + side, vsize)
         value = value.astype(BF16).astype(F32)
-        shifted[1, place, :] = value
-        shifted[0, place, :] = pltpu.roll(value * flags[place, 4:5], vsize - 1, 0)
-        shifted[2, place, :] = pltpu.roll(value * flags[place, 5:6], 1, 0)
+        acc[1, place, :] = value
+        acc[0, place, :] = pltpu.roll(value * flags[place, 4:5], vsize - 1, 0)
+        acc[2, place, :] = pltpu.roll(value * flags[place, 5:6], 1, 0)
 
     def nine_rows(start):
         for row_tap in range(3):
             source = pl.ds(start + side - side * (row_tap - 1), vsize)
             for col_tap in range(3):
                 tap = 3 * row_tap + col_tap
-                value = shifted[col_tap, source, :]
+                value = acc[col_tap, source, :]
                 if row_tap != 1:
                     column = 2 if row_tap == 0 else 3
                     value = value * flags[source, column : column + 1]
@@ -1350,8 +1166,9 @@
     def tap_back(stage, layer, offset, settle, begin_sums, now, span):
         index = 2 * layer + 1
         go = scatter(stage, 1)
+        if stage == 2:
+            mixed_copy.wait()
         tiles(rows, vsize, nine_rows)
-        have(f"second{layer}")
         spread_out(
             go,
             lambda place: spread[place, :],
@@ -1360,7 +1177,6 @@
             now,
             span,
         )
-        have(f"half{index}")
         for pair in range(2):
             left = two_of(hbuf.at[index], pair)
             for row_tap in range(3):
@@ -1410,7 +1226,7 @@
         now += 18
         slim_back(
             2 * layer,
-            lambda place: up_slim[place, :],
+            lambda place: z_slim[place, :],
             gain_b[2 * layer : 2 * layer + 1, :],
             shift_b[2 * layer : 2 * layer + 1, :],
             keep_slim,
@@ -1420,18 +1236,16 @@
             stage + 1,
             2 * layer,
             wf.at[layer],
-            f"first{layer}",
             first_row[layer],
             branch_more,
             now,
             15,
         ).drain()
 
-    have("hat_split")
     norm_back(
         wide_ex[1],
         lambda place: join([branch[place, :], bypass[place, :]]),
-        up_wide,
+        z_wide,
         hat_wide.at[1],
         join([gain_s[0:1, :], gain_s[1:2, :]]),
         join([shift_s[0:1, :], shift_s[1:2, :]]),
@@ -1440,7 +1254,6 @@
         keep_wide,
         108,
     )
-    have("split")
     split_go = scatter(6, 2)
 
     def split_terms(owner, chunk):
@@ -1473,7 +1286,6 @@
             split_go.mate_copy(2 * part + chunk).start()
     for chunk in range(2):
         split_terms(at.chan, chunk)
-    have("down_low")
     for owner in range(4):
         result = lax.dot_general(
             dbuf[rows * owner : rows * (owner + 1), :], dz_wide[...], along_dims, preferred_element_type=F32
@@ -1487,7 +1299,7 @@
 
     def wide_up(part, chunk):
         def give(start, value):
-            up_wide[
+            z_wide[
                 pl.ds(start + chunk * half_rows, vsize), LANES * part : LANES * (part + 1)
             ] = value
 
@@ -1505,14 +1317,13 @@
         moved = pltpu.roll(value * flags[place, 1:2], vsize - 1, 0)
         for half in range(2):
             lanes = slice(LANES * half, LANES * (half + 1))
-            shifted[half, place, :] = value[:, lanes]
-            shifted[2 + half, place, :] = moved[:, lanes]
-
-    have("hat_down")
+            acc[half, place, :] = value[:, lanes]
+            acc[2 + half, place, :] = moved[:, lanes]
+
     norm_back(
         wide_ex[0],
-        lambda place: up_wide[place, :],
-        up_wide,
+        lambda place: z_wide[place, :],
+        z_wide,
         hat_wide.at[0],
         gain_d[...],
         shift_d[...],
@@ -1529,13 +1340,12 @@
         for kind in range(2):
             for half in range(2):
                 lane = 256 * kind + LANES * half
-                spread[place, lane : lane + LANES] = shifted[2 * kind + half, here, :].astype(BF16)
+                spread[place, lane : lane + LANES] = acc[2 * kind + half, here, :].astype(BF16)
                 spread[place, 512 + lane : 512 + lane + LANES] = (
-                    shifted[2 * kind + half, below, :] * keep
+                    acc[2 * kind + half, below, :] * keep
                 ).astype(BF16)
 
     tiles(rows, vsize, four_rows)
-    have("features")
 
     def version(row_tap, col_tap):
         return 256 * (2 * (row_tap == 0) + (col_tap == 0))
@@ -1564,7 +1374,6 @@
             begin(sum_down.at[piece], dbuf.at[pl.ds(taken, room)], int(turn), down_out.at[piece], now)
             taken += room
             pause(now)
-    have("down")
 
     down_go = Scatter(
         at,
@@ -1572,10 +1381,10 @@
             lambda owner, phase: hbuf.at[phase, owner],
             lambda block, phase: jbuf.at[block, phase],
             lambda phase: rcross_d.at[phase],
-            lambda phase: across_d.at[phase],
+            lambda phase: feat.at[pl.ds(phase * rows, rows)],
         ),
-        send,
-        recv,
+        tsend,
+        trecv,
         base[0],
     )
     order = (3, 2, 1, 0)
@@ -1643,7 +1452,7 @@
         made.drain()
 
 
-def backward_call(batch_count, side, grad_in, flags, weights, kept, inverses, vectors):
+def section_call(batch_count, side, flags, vectors, feat, grad_in, weights):
     rows = grad_in.shape[0]
     wide = 2 * LANES
     hbm = pl.BlockSpec(memory_space=pl.ANY)
@@ -1653,13 +1462,18 @@
     bits = batch_count.bit_length() - 1
     near = list(range(bits))
     turned = [1, 0, *near[2:]] if bits > 1 else near
-    feat_rows = 2 * rows // side
     sums = [
         shape((1024, wide), BF16),
         shape((big_rows, LANES), BF16),
         shape((4608, wide), BF16),
     ]
+    slots = [
+        pltpu.VMEM((3, batch_count, 8, wide), F32),
+        pltpu.VMEM((5, batch_count, 8, LANES), F32),
+    ]
+    turns = [dma((3, batch_count)), dma((5, batch_count))]
     scratch = [
+        pltpu.VMEM(feat.shape, BF16),
         pltpu.VMEM((rows, wide), BF16),
         pltpu.VMEM((9, 512, wide), BF16),
         pltpu.VMEM((1024, wide), BF16),
@@ -1673,11 +1487,13 @@
         pltpu.VMEM((2, 4, rows, LANES), BF16),
         pltpu.VMEM((3, rows, wide), F32),
         pltpu.VMEM((5, rows, LANES), F32),
+        pltpu.VMEM((3, 8, wide), F32),
+        pltpu.VMEM((5, 8, LANES), F32),
+        pltpu.VMEM((4, rows + 2 * side, LANES), F32),
         pltpu.VMEM((rows, wide), F32),
         pltpu.VMEM((rows, LANES), F32),
         pltpu.VMEM((rows, LANES), F32),
         pltpu.VMEM((rows, LANES), F32),
-        pltpu.VMEM((4, rows + 2 * side, LANES), F32),
         pltpu.VMEM((rows, 9 * LANES), BF16),
         pltpu.VMEM((rows, wide), BF16),
         pltpu.VMEM((rows, LANES), BF16),
@@ -1686,40 +1502,36 @@
         pltpu.VMEM((2, 2, rows, LANES), BF16),
         pltpu.VMEM((2, rows, LANES), BF16),
         pltpu.VMEM((4, rows, LANES), BF16),
-        pltpu.VMEM((4, rows, LANES), BF16),
         *[pltpu.VMEM(one.shape, one.dtype) for one in sums],
-        *[
-            pltpu.VMEM((landing_rows(one.shape[0], batch_count), one.shape[1]), one.dtype)
-            for one in sums[:2]
-        ],
-        pltpu.VMEM((3, batch_count, 8, wide), F32),
-        pltpu.VMEM((5, batch_count, 8, LANES), F32),
-        dma((3, batch_count)),
-        dma((5, batch_count)),
-        dma((3, batch_count)),
-        dma((5, batch_count)),
+        pltpu.VMEM((landing_rows(big_rows, batch_count), LANES), BF16),
+        *slots,
+        *turns,
+        *turns,
+        dma((60,)),
+        dma((60,)),
         dma((72,)),
         dma((72,)),
         dma((15 * 2 * bits,)),
         dma((15 * 2 * bits,)),
-        dma((60,)),
-        dma((15,)),
+        dma((40,)),
+        dma((16,)),
     ]
     return pl.pallas_call(
-        functools.partial(backward_kernel, batch_count, side, (near, turned)),
+        functools.partial(section_kernel, batch_count, side, (near, turned)),
         out_shape=[
-            shape((feat_rows, 2 * side, LANES), F32),
+            shape((rows, wide), BF16),
+            shape((2 * rows // side, 2 * side, LANES), F32),
             shape((3, 8, wide), F32),
             shape((5, 8, LANES), F32),
             *sums,
         ],
-        in_specs=[hbm, vmem] + [hbm] * 6 + [hbm] * 6 + [vmem] * 2 + [vmem] * 10,
-        out_specs=[vmem] * 3 + [hbm] * 3,
+        in_specs=[vmem] * 11 + [hbm] * 8,
+        out_specs=[hbm] + [vmem] * 3 + [hbm] * 3,
         scratch_shapes=scratch,
         compiler_params=pltpu.CompilerParams(
-            collective_id=1, has_side_effects=True, vmem_limit_bytes=VMEM_LIMIT
+            collective_id=0, has_side_effects=True, vmem_limit_bytes=VMEM_LIMIT
         ),
-    )(grad_in, flags, *weights, *kept, *inverses, *vectors)
+    )(flags, *vectors, feat, grad_in, *weights)
 
 
 def local(
@@ -1770,18 +1582,14 @@
         row(gain_merge),
         row(shift_merge),
     )
-    mixed, *kept = forward_call(
+    mixed, feat_grad, vec_wide, vec_slim, merge, big, down = section_call(
         count,
         side,
-        features.reshape(-1, features.shape[2], features.shape[3]),
         flags,
+        vectors,
+        features.reshape(-1, features.shape[3]),
+        out_grad.reshape(-1, out_grad.shape[3]),
         weights,
-        vectors,
-    )
-    kept[1] = kept[1].reshape(-1, kept[1].shape[2])
-    grad_rows = out_grad.reshape(-1, out_grad.shape[3])
-    feat_grad, vec_wide, vec_slim, merge, big, down = backward_call(
-        count, side, grad_rows, flags, weights, kept[:6], kept[6:], vectors
     )
     rows = w_trans.shape[0]
     two = second_row[0]

time: 407 us -> 400 us (0.983)
  Pallas kernels: 385 us -> 378 us
    pallas_call x2 -> x1, Pallas kernels: 385 us -> 378 us  [section_call(): pl.pallas_call(functools.partial(section_kernel, batch_count, side, (near...]
where the time goes in v2:
time: 400 us; the launch traced here: 399 us
  Pallas kernels  378 us (94%)
  other arithmetic  11.2 us (3%)
  local copies, waits for them, and re-layouts  9.52 us (2%)
    pallas_call x1, Pallas kernels, section_call(): pl.pallas_call(functools.partial(section_kernel, batch_count, side, (near...  378 us

profile of v2, /device:TPU:0, one launch (start us, length us, event | category | flops | bytes accessed | tf_op | source)
XLA Modules:
  0.0 399.4 jit_solution(1842896888401401257)
XLA Ops:
  0.7 1.0 slice_reduce_fusion
  1.9 0.1 fusion.1
  2.0 0.1 stack_reshape.18
  2.1 0.1 stack_reshape.19
  2.2 0.1 and_convert_fusion
  2.4 0.1 stack_reshape.20
  2.6 0.1 stack_reshape.21
  2.7 0.1 stack_reshape.22
  2.8 0.1 stack_reshape.23
  2.9 0.2 copy.43
  3.2 0.9 pad.4.flags
  4.1 378.0 %shard_map.322 = (bf16[1152,256]{1,0:T(8,128)(2,1)}, f32[96,48,128]{2,1,0:T(8,128)}, f32[3,8,256]{2,1,0:T(8,128)}, f32[5,8,128]{2,1,0:T(8,128)}, bf16[1024,256]{...) custom-call(f32[1200,8]{1,0:T(8,128)} %pad.4.flags, f32[1,256]{1,0:T(1,128)} %bitcast.63, ...), custom_call_target="tpu_custom_call" | custom-call | tf_op jit(solution)/shard_map/pallas_call | solution.py:1519
  382.0 4.4 %convert.7 = f32[3,3,512,256]{3,2,1,0:T(8,128)} convert(bf16[3,3,512,256]{3,2,1,0:T(8,128)(2,1)} %bitcast.52) | non-fusion elementwise | flops 1179648 | bytes 7077888 | tf_op jit(solution)/shard_map/convert_element_type | solution.py:1601
  386.5 1.4 fusion.2
  387.9 1.0 convert.8
  389.0 0.7 slice_convert_fusion
  389.7 0.8 maximum_convert_fusion
  390.5 0.2 slice.88
  390.7 2.7 convert.9
  393.4 1.5 fusion.3
  394.9 1.3 slice_bitcast_fusion.6
  396.2 1.0 convert_element_type.47
  397.2 0.8 copy.46
  398.0 1.4 copy.47
  (25 shorter events, 0.6 us)
Async XLA Ops:
  382.0 5.8 %copy-start = (bf16[12800,128]{1,0:T(8,128)(2,1)S(1)}, bf16[12800,128]{1,0:T(8,128)(2,1)}, u32[]{:S(2)}) copy-start(bf16[12800,128]{1,0:T(8,128)(2,1)} %get-tuple-element.29) | copy-start | bytes 9830404
  390.7 5.4 %copy-start.3 = (bf16[1024,256]{1,0:T(8,128)(2,1)S(1)}, bf16[1024,256]{1,0:T(8,128)(2,1)}, u32[]{:S(2)}) copy-start(bf16[1024,256]{1,0:T(8,128)(2,1)} %get-tuple-element.31) | copy-start | bytes 1572868
  390.7 6.5 %copy-start.2 = (bf16[1152,256]{1,0:T(8,128)(2,1)S(1)}, bf16[1152,256]{1,0:T(8,128)(2,1)}, u32[]{:S(2)}) copy-start(bf16[1152,256]{1,0:T(8,128)(2,1)} %get-tuple-element.25) | copy-start | bytes 1769476
  393.4 4.6 %copy-start.1 = (f32[96,48,128]{2,1,0:T(8,128)S(1)}, f32[96,48,128]{2,1,0:T(8,128)}, u32[]{:S(2)}) copy-start(f32[96,48,128]{2,1,0:T(8,128)} %get-tuple-element.26) | copy-start | bytes 7077892

commit v3 on v2

--- a/solution.py
+++ b/solution.py
@@ -189,6 +189,9 @@
 
 def join(halves):
     return jnp.concatenate(halves, axis=1)
+
+
+CHUNKS = 4
 
 
 class Norms:
@@ -496,6 +499,9 @@
     me = at.chan
     rows = z_wide.shape[0]
     half_rows = rows // 2
+    bsize = 192
+    parts = CHUNKS
+    part_rows = rows // parts
     pixels = rows * batch_count
     area = side * side
 
@@ -538,18 +544,18 @@
         return made
 
     def by_half(ref):
-        return lambda owner, chunk: ref.at[owner, pl.ds(chunk * half_rows, half_rows)]
+        return lambda owner, chunk: ref.at[owner, pl.ds(chunk * part_rows, part_rows)]
 
     feat_go = gather(lambda owner, phase: fbuf.at[owner, phase], 4)
     def down_rows(owner, start, size):
         return pl.ds(pl.multiple_of(owner * rows + start, 16), size)
 
     down_go = gather(
-        lambda owner, chunk: dbuf.at[down_rows(owner, chunk * half_rows, half_rows)], 2
+        lambda owner, chunk: dbuf.at[down_rows(owner, chunk * part_rows, part_rows)], parts
     )
-    half_go = [gather(by_half(hbuf.at[index]), 2) for index in range(5)]
-    side_go = gather(by_half(jbuf.at[1]), 2)
-    top_go = gather(by_half(jbuf.at[0]), 2)
+    half_go = [gather(by_half(hbuf.at[index]), parts) for index in range(5)]
+    side_go = gather(by_half(jbuf.at[1]), parts)
+    top_go = gather(by_half(jbuf.at[0]), parts)
     wide_ex = [
         Exchange(at, slots_wide.at[index], wide_sem.at[index], wide_rsem.at[index])
         for index in range(3)
@@ -645,12 +651,12 @@
             _, top = mish_parts(before)
             give(start, before * (top / (top + 2.0)))
 
-        for chunk in range(2):
+        for chunk in range(parts):
 
             def inner(start):
-                body(start + chunk * half_rows)
-
-            tiles(half_rows, vsize, inner)
+                body(start + chunk * part_rows)
+
+            tiles(part_rows, vsize, inner)
             begin(chunk)
 
     def keep_down(start, value):
@@ -662,13 +668,13 @@
     )
     have("split")
 
-    msize = 192
+    msize = max(size for size in (288, 192) if part_rows % size == 0)
 
     def split_block(owner, chunk, first):
         def body(start):
-            place = pl.ds(start + chunk * half_rows, msize)
+            place = pl.ds(start + chunk * part_rows, msize)
             part = jnp.dot(
-                dbuf[down_rows(owner, start + chunk * half_rows, msize), :],
+                dbuf[down_rows(owner, start + chunk * part_rows, msize), :],
                 ws[pl.ds(pl.multiple_of(owner * 256, 256), 256), :],
                 preferred_element_type=F32,
             )
@@ -677,17 +683,17 @@
             else:
                 z_wide[place, :] += part
 
-        tiles(half_rows, msize, body)
-
-    for chunk in range(2):
+        tiles(part_rows, msize, body)
+
+    for chunk in range(parts):
         split_block(me, chunk, True)
-    for chunk in range(2):
+    for chunk in range(parts):
         down_go.wait_mate(chunk)
         split_block(at.mate, chunk, False)
-    for chunk in range(2):
+    for chunk in range(parts):
         down_go.forward(chunk)
         split_block(at.cross, chunk, False)
-    for chunk in range(2):
+    for chunk in range(parts):
         down_go.wait_far(chunk)
         split_block(at.far, chunk, False)
 
@@ -707,7 +713,7 @@
         keep_split,
         half_go[0].start,
     )
-    for chunk in range(2):
+    for chunk in range(parts):
         side_go.start(chunk)
 
     def two_of(ref, pair, place):
@@ -715,7 +721,7 @@
 
     def thin_pair(source, weight, pair, chunk, first):
         def body(start):
-            place = pl.ds(start + chunk * half_rows, msize)
+            place = pl.ds(start + chunk * part_rows, msize)
             part = jnp.dot(
                 two_of(source, pair, place),
                 weight[pl.ds(pl.multiple_of(pair * 256, 256), 256), :],
@@ -726,22 +732,22 @@
             else:
                 z_slim[place, :] += part
 
-        tiles(half_rows, msize, body)
+        tiles(part_rows, msize, body)
 
     def thin_conv(index, weight):
         source, go = hbuf.at[index], half_go[index]
-        for chunk in range(2):
+        for chunk in range(parts):
             go.wait_mate(chunk)
             thin_pair(source, weight, at.pair, chunk, True)
-        for chunk in range(2):
+        for chunk in range(parts):
             go.forward(chunk)
-        for chunk in range(2):
+        for chunk in range(parts):
             go.wait_far(chunk)
             thin_pair(source, weight, 1 - at.pair, chunk, False)
 
     def tap_pair(source, weight, pair, chunk):
         def body(start):
-            begin = start + chunk * half_rows
+            begin = start + chunk * part_rows
             part = jnp.dot(
                 two_of(source, pair, pl.ds(begin, msize)),
                 weight[pl.ds(pl.multiple_of(pair * 256, 256), 256), :],
@@ -757,17 +763,17 @@
                         piece = piece * flags[place, column : column + 1]
                     acc[col_tap, place, :] += piece
 
-        tiles(half_rows, msize, body)
+        tiles(part_rows, msize, body)
 
     def tap_conv(index, weight):
         source, go = hbuf.at[index], half_go[index]
         acc[0:3] = jnp.zeros((3, *acc.shape[1:]), F32)
-        for chunk in range(2):
+        for chunk in range(parts):
             go.wait_mate(chunk)
             tap_pair(source, weight, at.pair, chunk)
-        for chunk in range(2):
+        for chunk in range(parts):
             go.forward(chunk)
-        for chunk in range(2):
+        for chunk in range(parts):
             go.wait_far(chunk)
             tap_pair(source, weight, 1 - at.pair, chunk)
 
@@ -818,7 +824,7 @@
             half_go[2 * layer + 2].start,
         )
         if layer == 0:
-            for chunk in range(2):
+            for chunk in range(parts):
                 side_go.forward(chunk)
     have("trans")
     thin_conv(4, wt)
@@ -832,7 +838,7 @@
 
     def merge_pair(part_index, pair, chunk, first):
         def body(start):
-            place = pl.ds(start + chunk * half_rows, msize)
+            place = pl.ds(start + chunk * part_rows, msize)
             part = jnp.dot(
                 two_of(jbuf.at[part_index], pair, place),
                 wm[pl.ds(pl.multiple_of(part_index * 512 + pair * 256, 256), 256), :],
@@ -843,20 +849,20 @@
             else:
                 z_wide[place, :] += part
 
-        tiles(half_rows, msize, body)
-
-    for chunk in range(2):
+        tiles(part_rows, msize, body)
+
+    for chunk in range(parts):
         side_go.wait_mate(chunk)
         merge_pair(1, at.pair, chunk, True)
-    for chunk in range(2):
+    for chunk in range(parts):
         side_go.wait_far(chunk)
         merge_pair(1, 1 - at.pair, chunk, False)
-    for chunk in range(2):
+    for chunk in range(parts):
         top_go.wait_mate(chunk)
         merge_pair(0, at.pair, chunk, False)
-    for chunk in range(2):
+    for chunk in range(parts):
         top_go.forward(chunk)
-    for chunk in range(2):
+    for chunk in range(parts):
         top_go.wait_far(chunk)
         merge_pair(0, 1 - at.pair, chunk, False)
 
@@ -1007,14 +1013,14 @@
         def body(start):
             begin_at = start + chunk * half_rows
             terms = lax.dot_general(
-                left(pl.ds(begin_at, msize)), weight, across_dims, preferred_element_type=F32
+                left(pl.ds(begin_at, bsize)), weight, across_dims, preferred_element_type=F32
             ).astype(BF16)
             for step in range(2):
-                pbuf[part, 2 * pair + step, pl.ds(begin_at, msize), :] = terms[
+                pbuf[part, 2 * pair + step, pl.ds(begin_at, bsize), :] = terms[
                     :, LANES * step : LANES * (step + 1)
                 ]
 
-        tiles(half_rows, msize, body)
+        tiles(half_rows, bsize, body)
 
     def pair_rows(pair, offset=0):
         return pl.ds(pl.multiple_of(offset + pair * 256, 256), 256)
@@ -1258,7 +1264,7 @@
 
     def split_terms(owner, chunk):
         def body(start):
-            place = pl.ds(start + chunk * half_rows, msize)
+            place = pl.ds(start + chunk * half_rows, bsize)
             terms = lax.dot_general(
                 dz_wide[place, :],
                 ws[pl.ds(pl.multiple_of(owner * 256, 256), 256), :],
@@ -1268,7 +1274,7 @@
             for part in range(2):
                 pbuf[part, owner, place, :] = terms[:, LANES * part : LANES * (part + 1)]
 
-        tiles(half_rows, msize, body)
+        tiles(half_rows, bsize, body)
 
     for chunk in range(2):
         split_terms(at.far, chunk)
@@ -1394,7 +1400,7 @@
         col_taps = (0, 2) if phase % 2 else (1,)
 
         def body(start):
-            place = pl.ds(start, msize)
+            place = pl.ds(start, bsize)
             total = None
             for row_tap in row_taps:
                 for col_tap in col_taps:
@@ -1410,7 +1416,7 @@
             for step in range(2):
                 hbuf[phase, 2 * pair + step, place, :] = terms[:, LANES * step : LANES * (step + 1)]
 
-        tiles(rows, msize, body)
+        tiles(rows, bsize, body)
 
     for phase in order:
         feature_terms(phase, 1 - at.pair)
@@ -1507,8 +1513,8 @@
         *slots,
         *turns,
         *turns,
-        dma((60,)),
-        dma((60,)),
+        dma((110,)),
+        dma((110,)),
         dma((72,)),
         dma((72,)),
         dma((15 * 2 * bits,)),

time: 400 us -> 396 us (0.990)
  Pallas kernels: 378 us -> 374 us
where the time goes in v3:
time: 396 us
  Pallas kernels  374 us (94%)
  other arithmetic  11.2 us (3%)
  local copies, waits for them, and re-layouts  9.52 us (2%)
    pallas_call x1, Pallas kernels, section_call(): pl.pallas_call(functools.partial(section_kernel, batch_count, side, (near...  374 us

profile of v3, /device:TPU:0, one launch (start us, length us, event | category | flops | bytes accessed | tf_op | source)
XLA Modules:
  0.0 395.9 jit_solution(9415865916328599303)
XLA Ops:
  0.7 1.0 slice_reduce_fusion
  1.9 0.1 fusion.1
  2.0 0.1 stack_reshape.18
  2.1 0.1 stack_reshape.19
  2.2 0.1 and_convert_fusion
  2.4 0.1 stack_reshape.20
  2.6 0.1 stack_reshape.21
  2.7 0.1 stack_reshape.22
  2.8 0.1 stack_reshape.23
  2.9 0.2 copy.43
  3.2 0.9 pad.4.flags
  4.1 374.4 %shard_map.322 = (bf16[1152,256]{1,0:T(8,128)(2,1)}, f32[96,48,128]{2,1,0:T(8,128)}, f32[3,8,256]{2,1,0:T(8,128)}, f32[5,8,128]{2,1,0:T(8,128)}, bf16[1024,256]{...) custom-call(f32[1200,8]{1,0:T(8,128)} %pad.4.flags, f32[1,256]{1,0:T(1,128)} %bitcast.63, ...), custom_call_target="tpu_custom_call" | custom-call | tf_op jit(solution)/shard_map/pallas_call | solution.py:1525
  378.5 4.4 %convert.7 = f32[3,3,512,256]{3,2,1,0:T(8,128)} convert(bf16[3,3,512,256]{3,2,1,0:T(8,128)(2,1)} %bitcast.52) | non-fusion elementwise | flops 1179648 | bytes 7077888 | tf_op jit(solution)/shard_map/convert_element_type | solution.py:1607
  382.9 1.4 fusion.2
  384.4 1.0 convert.8
  385.4 0.7 slice_convert_fusion
  386.1 0.8 maximum_convert_fusion
  387.0 0.2 slice.88
  387.2 2.7 convert.9
  389.9 1.5 fusion.3
  391.3 1.3 slice_bitcast_fusion.6
  392.6 1.0 convert_element_type.47
  393.7 0.8 copy.46
  394.5 1.4 copy.47
  (25 shorter events, 0.6 us)
Async XLA Ops:
  378.5 5.8 %copy-start = (bf16[12800,128]{1,0:T(8,128)(2,1)S(1)}, bf16[12800,128]{1,0:T(8,128)(2,1)}, u32[]{:S(2)}) copy-start(bf16[12800,128]{1,0:T(8,128)(2,1)} %get-tuple-element.29) | copy-start | bytes 9830404
  387.2 5.4 %copy-start.3 = (bf16[1024,256]{1,0:T(8,128)(2,1)S(1)}, bf16[1024,256]{1,0:T(8,128)(2,1)}, u32[]{:S(2)}) copy-start(bf16[1024,256]{1,0:T(8,128)(2,1)} %get-tuple-element.31) | copy-start | bytes 1572868
  387.2 6.5 %copy-start.2 = (bf16[1152,256]{1,0:T(8,128)(2,1)S(1)}, bf16[1152,256]{1,0:T(8,128)(2,1)}, u32[]{:S(2)}) copy-start(bf16[1152,256]{1,0:T(8,128)(2,1)} %get-tuple-element.25) | copy-start | bytes 1769476
  389.9 4.6 %copy-start.1 = (f32[96,48,128]{2,1,0:T(8,128)S(1)}, f32[96,48,128]{2,1,0:T(8,128)}, u32[]{:S(2)}) copy-start(f32[96,48,128]{2,1,0:T(8,128)} %get-tuple-element.26) | copy-start | bytes 7077892

commit v4 on v3

--- a/solution.py
+++ b/solution.py
@@ -408,7 +408,9 @@
 second_row = (512, 5120)
 trans_row = 9728
 split_row = 10752
-tap_ends = (2, 5, 7, 9)
+tap_ends = (2, 4, 6, 8, 9)
+late_parts = ((0, 1536, 0), (1536, 1536, 1), (3072, 2048, 0))
+split_parts = ((0, 1536, 0), (1536, 1024, 1))
 big_rows = 12800
 
 
@@ -1202,12 +1204,12 @@
         go.drain()
 
     def late_sums(now):
-        begin_rows(second_row[1], 2560, 0, now)
-        begin_rows(second_row[1] + 2560, 2560, 1, now)
+        for low, size, order in late_parts:
+            begin_rows(second_row[1] + low, size, order, now)
 
     def early_sums(now):
-        begin_rows(0, 2560, 0, now)
-        begin_rows(2560, 2560, 1, now)
+        for low, size, order in late_parts:
+            begin_rows(low, size, order, now)
 
     for layer in (1, 0):
         stage = 2 if layer == 1 else 4
@@ -1300,7 +1302,8 @@
             sum_big[pl.ds(split_row + 1024 * part + 256 * owner, 256), :] = result[
                 :, LANES * part : LANES * (part + 1)
             ]
-    begin_rows(first_row[0], 2560, 0, 122)
+    for low, size, order in split_parts:
+        begin_rows(first_row[0] + low, size, order, 122)
     pause(122)
 
     def wide_up(part, chunk):

time: 396 us -> 383 us (0.967)
  Pallas kernels: 374 us -> 361 us
    pallas_call x1, Pallas kernels: 374 us -> 361 us  [section_call(): pl.pallas_call(functools.partial(section_kernel, batch_count, side, (near...]
where the time goes in v4:
time: 383 us
  Pallas kernels  361 us (94%)
  other arithmetic  11.2 us (3%)
  local copies, waits for them, and re-layouts  9.52 us (2%)
    pallas_call x1, Pallas kernels, section_call(): pl.pallas_call(functools.partial(section_kernel, batch_count, side, (near...  361 us

profile of v4, /device:TPU:0, one launch (start us, length us, event | category | flops | bytes accessed | tf_op | source)
XLA Modules:
  0.0 382.6 jit_solution(13805740619040470196)
XLA Ops:
  0.7 1.0 slice_reduce_fusion
  1.9 0.1 fusion.1
  2.0 0.1 stack_reshape.18
  2.1 0.1 stack_reshape.19
  2.2 0.1 and_convert_fusion
  2.4 0.1 stack_reshape.20
  2.6 0.1 stack_reshape.21
  2.7 0.1 stack_reshape.22
  2.8 0.1 stack_reshape.23
  2.9 0.2 copy.43
  3.2 0.9 pad.4.flags
  4.1 361.1 %shard_map.322 = (bf16[1152,256]{1,0:T(8,128)(2,1)}, f32[96,48,128]{2,1,0:T(8,128)}, f32[3,8,256]{2,1,0:T(8,128)}, f32[5,8,128]{2,1,0:T(8,128)}, bf16[1024,256]{...) custom-call(f32[1200,8]{1,0:T(8,128)} %pad.4.flags, f32[1,256]{1,0:T(1,128)} %bitcast.63, ...), custom_call_target="tpu_custom_call" | custom-call | tf_op jit(solution)/shard_map/pallas_call | solution.py:1528
  365.2 4.4 %convert.7 = f32[3,3,512,256]{3,2,1,0:T(8,128)} convert(bf16[3,3,512,256]{3,2,1,0:T(8,128)(2,1)} %bitcast.52) | non-fusion elementwise | flops 1179648 | bytes 7077888 | tf_op jit(solution)/shard_map/convert_element_type | solution.py:1610
  369.7 1.4 fusion.2
  371.1 1.0 convert.8
  372.1 0.7 slice_convert_fusion
  372.9 0.8 maximum_convert_fusion
  373.7 0.2 slice.88
  373.9 2.7 convert.9
  376.6 1.5 fusion.3
  378.1 1.3 slice_bitcast_fusion.6
  379.3 1.0 convert_element_type.47
  380.4 0.8 copy.46
  381.2 1.4 copy.47
  (25 shorter events, 0.6 us)
Async XLA Ops:
  365.2 5.8 %copy-start = (bf16[12800,128]{1,0:T(8,128)(2,1)S(1)}, bf16[12800,128]{1,0:T(8,128)(2,1)}, u32[]{:S(2)}) copy-start(bf16[12800,128]{1,0:T(8,128)(2,1)} %get-tuple-element.29) | copy-start | bytes 9830404
  373.9 5.4 %copy-start.3 = (bf16[1024,256]{1,0:T(8,128)(2,1)S(1)}, bf16[1024,256]{1,0:T(8,128)(2,1)}, u32[]{:S(2)}) copy-start(bf16[1024,256]{1,0:T(8,128)(2,1)} %get-tuple-element.31) | copy-start | bytes 1572868
  373.9 6.5 %copy-start.2 = (bf16[1152,256]{1,0:T(8,128)(2,1)S(1)}, bf16[1152,256]{1,0:T(8,128)(2,1)}, u32[]{:S(2)}) copy-start(bf16[1152,256]{1,0:T(8,128)(2,1)} %get-tuple-element.25) | copy-start | bytes 1769476
  376.6 4.6 %copy-start.1 = (f32[96,48,128]{2,1,0:T(8,128)S(1)}, f32[96,48,128]{2,1,0:T(8,128)}, u32[]{:S(2)}) copy-start(f32[96,48,128]{2,1,0:T(8,128)} %get-tuple-element.26) | copy-start | bytes 7077892
